TPU v7x, 1024 devices: a whole 4x4x32 slice. The times are simulated.
1024 devices in a mesh: wide: 32 (over z_lo, core), narrow: 32 (over y, x, z_hi).
Axes of the slice: x: 4, y: 4, z: 32 (z_hi: 2, z_lo: 16; z = z_hi * 16 + z_lo), core: 2. Of those that a mesh axis runs over, the one named last changes fastest.
Arguments:
- left_values: bfloat16 [32, 64, 128, 128], P('wide', 'narrow'), may hold values from -6 to 6
- right_values: bfloat16 [64, 32, 128, 128], P('wide', 'narrow'), may hold values from -0.25 to 0.25
- stack_left: int32 [32, 32, 64, 4], P('wide', 'narrow'), may hold values from 0 to 63
- stack_right: int32 [32, 32, 64, 4], P('wide', 'narrow'), may hold values from 0 to 63
- stack_slot: int32 [32, 32, 64], P('wide', 'narrow'), may hold values from 0 to 7
- stack_count: int32 [32, 32], P('wide', 'narrow'), may hold values from 1 to 64, as said below
Outputs:
- product: float32 [32, 256, 128, 128], P('wide', 'narrow')
Inputs may be any that keep to these rules, and one draw needn't show every extreme that they name: Stacks at positions stack_count[w, n] and beyond are unused; some entry equals 64.
All inputs are finite; a program needn't handle non-finite values.
Results may differ from a plain program's by a relative error of at most 0.0003.
Values may be sent and summed in bfloat16 or wider, within the bound.
No kernel may reach another device: no remote copies, remote signals or barrier semaphores. Data moves between devices by JAX's collectives and lax.ppermute only.
A program may use at most 32 MiB of HBM per device.

v0:
```python
import jax
import jax.numpy as jnp
from jax import lax
from jax.sharding import PartitionSpec as P

CSLOT = 8


def run_stacks(total, left_rows, right_cols, lefts, rights, slots, lower, upper):
    stacks = lefts.shape[0]
    group = min(16, stacks)
    slot_count = total.shape[0]

    def step(index, acc):
        start = index * group
        pick_a = lax.dynamic_slice_in_dim(lefts, start, group, 0)
        pick_b = lax.dynamic_slice_in_dim(rights, start, group, 0)
        pick_c = lax.dynamic_slice_in_dim(slots, start, group, 0)
        chosen_a = left_rows[pick_a]
        chosen_b = right_cols[pick_b]
        sums = jnp.einsum("gsij,gsjk->gik", chosen_a, chosen_b, preferred_element_type=jnp.float32)
        places = start + jnp.arange(group, dtype=jnp.int32)
        live = (places >= lower) & (places < upper)
        match = (pick_c[None, :] == jnp.arange(slot_count, dtype=jnp.int32)[:, None]) & live[
            None, :
        ]
        onehot = jnp.where(match, 1.0, 0.0).astype(jnp.float32)
        return acc + jnp.einsum("cg,gij->cij", onehot, sums, precision=lax.Precision.HIGHEST)

    first = lower // group
    last = (upper + group - 1) // group
    return lax.fori_loop(first, last, step, total)


def body(left_values, right_values, stack_left, stack_right, stack_slot, stack_count):
    left_rows = lax.all_gather(left_values, "narrow", axis=1, tiled=True)[0]
    right_cols = lax.all_gather(right_values, "wide", axis=0, tiled=True)[:, 0]
    block_size = left_values.shape[2]
    empty = jnp.zeros((CSLOT, block_size, block_size), jnp.float32)
    own_left = stack_left[0, 0]
    own_right = stack_right[0, 0]
    own_slot = stack_slot[0, 0]
    count = stack_count[0, 0]
    total = run_stacks(
        empty, left_rows, right_cols, own_left, own_right, own_slot, jnp.int32(0), count
    )
    return total[None]


def solution(mesh):
    return jax.shard_map(
        body,
        mesh=mesh,
        in_specs=(
            P("wide", "narrow", None, None),
            P("wide", "narrow", None, None),
            P("wide", "narrow", None, None),
            P("wide", "narrow", None, None),
            P("wide", "narrow", None),
            P("wide", "narrow"),
        ),
        out_specs=P("wide", "narrow", None, None),
        check_vma=False,
    )
```

profile of v0, /device:TPU:1, one launch (start us, length us, event | category | flops | bytes accessed | tf_op | source)
XLA Modules:
  0.0 597.6 jit_solution(925218228985154032)
XLA Ops:
  6.5 0.7 all-gather.3.cloned.1.call-update
  7.3 0.7 all-gather.5.cloned.1.call-update
  8.7 0.8 copy.16
  9.4 0.8 copy.18
  10.2 222.5 %all-gather.3.cloned.1.call-done = bf16[1,64,128,128]{3,2,0,1:T(8,128)(2,1)} async-done(((bf16[1,2,128,128]{3,2,0,1:T(8,128)(2,1)}), bf16[1,64,128,128]{3,2,0,1:T(8,128)(2,1)}) %all-gather.3.cloned.1.call-update) | async-done | bytes 2097168 | tf_op jit(solution)/shard_map/all_gather | solution.py:36
  232.7 311.0 %all-gather.5.cloned.1.call-done = bf16[64,1,128,128]{3,2,1,0:T(8,128)(2,1)} async-done(((bf16[2,1,128,128]{3,2,1,0:T(8,128)(2,1)}), bf16[64,1,128,128]{3,2,1,0:T(8,128)(2,1)}) %all-gather.5.cloned.1.call-update) | async-done | bytes 2097168 | tf_op jit(solution)/shard_map/all_gather | solution.py:37
  543.7 46.1 %while.10 = (s32[]{:T(128)}, f32[8,128,128]{2,0,1:T(8,128)S(1)}, s32[]{:T(128)}, s32[64]{0:T(128)}, s32[]{:T(128)}, /*index=5*/s32[64,4]{1,0:T(8,128)S(1)}, bf16...) while((s32[]{:T(128)}, f32[8,128,128]{2,0,1:T(8,128)S(1)}, ...), condition=%wide.region_1.2_spmd, body=%wide.region_0.1_spmd.sunk | while | flops 293735232 | bytes 15740315 | solution.py:32
  543.7 0.7 compare_and_fusion.2
  544.4 0.7 dynamic_slice.14
  545.3 2.5 gather_fusion
  547.9 3.7 gather_fusion.1
  551.6 2.3 convolution_bitcast_fusion.2
  553.9 1.3 convolution_add_fusion.2
  555.3 0.7 compare_and_fusion.2
  555.9 0.7 dynamic_slice.14
  556.9 2.5 gather_fusion
  559.4 3.7 gather_fusion.1
  563.2 2.3 convolution_bitcast_fusion.2
  565.5 1.3 convolution_add_fusion.2
  566.8 0.7 compare_and_fusion.2
  567.5 0.7 dynamic_slice.14
  568.4 2.5 gather_fusion
  571.0 3.7 gather_fusion.1
  574.7 2.3 convolution_bitcast_fusion.2
  577.0 1.3 convolution_add_fusion.2
  578.3 0.7 compare_and_fusion.2
  579.0 0.7 dynamic_slice.14
  579.9 2.5 gather_fusion
  582.5 3.7 gather_fusion.1
  586.2 2.3 convolution_bitcast_fusion.2
  588.5 1.3 convolution_add_fusion.2
  589.9 0.9 copy.24
  (23 shorter events, 0.8 us)
Async XLA Ops:
  6.5 226.2 %all-gather.3.cloned.1.call-start = ((), (), s32[]{:S(2)}) async-start(), calls=%async_computation | async-start | bytes 2162688 | tf_op jit(solution)/shard_map/all_gather | solution.py:36
  7.3 536.4 %all-gather.5.cloned.1.call-start = ((), (), s32[]{:S(2)}) async-start(), calls=%async_computation.1 | async-start | bytes 2162688 | tf_op jit(solution)/shard_map/all_gather | solution.py:37
Sparse Core Ops, SparseCore 0:
  13.2 219.4 all-gather.2
  235.3 308.2 all-gather.4
where the time goes:
time: 598 us
  waiting for transfers between devices  535 us (89%)
  local copies, waits for them, and re-layouts  31.2 us (5%)
  matrix products  14.4 us (2%)
  between operations  14.1 us (2%)
    all_gather x1, waiting for transfers between devices, body(): right_cols = lax.all_gather(right_values, 'wide', axis=0, tiled=True)[:, 0]  311 us
    all_gather x1, waiting for transfers between devices, body(): left_rows = lax.all_gather(left_values, 'narrow', axis=1, tiled=True)[0]  222 us
    gather x4, local copies, waits for them, and re-layouts, step(): chosen_b = right_cols[pick_b]  14.9 us
  transfers between devices with their start and end apart: 2, of which 2 were waited for; matrix products, arithmetic and copies ran while one was open for 0% of the time, Pallas kernels for 0%

commit v1 on v0

v1 whole, which is shorter than its diff:
```python
import jax
import jax.numpy as jnp
from jax import lax
from jax.experimental import pallas as pl
from jax.experimental.pallas import tpu as pltpu
from jax.sharding import Mesh
from jax.sharding import PartitionSpec as P

CSLOT = 8
UNROLL = 8
Z_HI, Z_LO = 4, 4
AXES = ("za", "zb", "core", "y", "x", "zh")
SIZES = (Z_HI, Z_LO, 2, 4, 4, 2)


def swap(value, axis, size, bits):
    return lax.ppermute(value, axis, [(i, i ^ bits) for i in range(size)])


def gather_plane(value):
    spread = jnp.broadcast_to(value[None], (16,) + value.shape)
    return lax.all_to_all(spread, ("y", "x"), split_axis=0, concat_axis=0, tiled=True)


def stacks_kernel(meta, own_h, far_h, a_h, b_h, ca_h, cb_h, out, left, right, sems):
    copies = [
        pltpu.make_async_copy(src, dst, sems.at[i])
        for i, (src, dst) in enumerate(
            (
                (own_h, left.at[pl.ds(0, 32)]),
                (far_h, left.at[pl.ds(32, 32)]),
                (a_h, right.at[pl.ds(0, 8)]),
                (b_h, right.at[pl.ds(8, 24)]),
                (ca_h, right.at[pl.ds(32, 8)]),
                (cb_h, right.at[pl.ds(40, 24)]),
            )
        )
    ]
    for copy in copies:
        copy.start()
    out[...] = jnp.zeros_like(out)
    za, zb, core, half = meta[577], meta[578], meta[579], meta[580]
    count = meta[576]

    def left_at(slot):
        place = ((slot >> 2) << 1) + (slot & 1)
        return place + ((((slot >> 1) & 1) ^ half) << 5)

    def right_at(slot):
        far = (slot >> 4) ^ za
        far = ((far & 1) << 1) + (far >> 1)
        near = ((slot >> 2) & 3) ^ zb
        other = ((slot >> 1) & 1) ^ core
        return (other << 5) + (near << 3) + (far << 1) + (slot & 1)

    def stack_sum(t):
        lefts = [left[left_at(meta[4 * t + g])] for g in range(4)]
        rights = [right[right_at(meta[256 + 4 * t + g])] for g in range(4)]
        return jnp.dot(
            jnp.concatenate(lefts, 1),
            jnp.concatenate(rights, 0),
            preferred_element_type=jnp.float32,
        )

    for copy in copies:
        copy.wait()

    def add(first, width):
        sums = [stack_sum(first + u) for u in range(width)]
        for u in range(width):
            slot = meta[512 + first + u]
            out[slot] = out[slot] + sums[u]

    def wide_step(i, carry):
        add(i * UNROLL, UNROLL)
        return carry

    def single_step(t, carry):
        add(t, 1)
        return carry

    groups = count // UNROLL
    lax.fori_loop(0, groups, wide_step, 0)
    lax.fori_loop(groups * UNROLL, count, single_step, 0)


def body(left_values, right_values, stack_left, stack_right, stack_slot, stack_count):
    own_left = left_values[0]
    own_right = right_values[:, 0]
    places = [lax.axis_index(a) for a in ("za", "zb", "core", "zh")]
    meta = jnp.concatenate(
        [
            stack_left.reshape(-1),
            stack_right.reshape(-1),
            stack_slot.reshape(-1),
            stack_count.reshape(-1),
            jnp.stack(places).astype(jnp.int32),
        ]
    )
    right_8 = swap(own_right, "za", Z_HI, 2)
    far_left = swap(own_left, "zh", 2, 1)
    pair = jnp.concatenate([own_right, right_8], 0)
    right_4 = swap(pair, "za", Z_HI, 1)
    plane_own = gather_plane(own_left)
    a = jnp.concatenate([pair, right_4], 0)
    b = jnp.concatenate([swap(a, "zb", Z_LO, k) for k in (1, 2, 3)], 0)
    plane_far = gather_plane(far_left)
    ca = swap(a, "core", 2, 1)
    cb = swap(b, "core", 2, 1)
    block = own_left.shape[1]
    return pl.pallas_call(
        stacks_kernel,
        out_shape=jax.ShapeDtypeStruct((CSLOT, block, block), jnp.float32),
        in_specs=[pl.BlockSpec(memory_space=pltpu.SMEM)]
        + [pl.BlockSpec(memory_space=pl.ANY)] * 6,
        out_specs=pl.BlockSpec(memory_space=pltpu.VMEM),
        scratch_shapes=[
            pltpu.VMEM((64, block, block), jnp.bfloat16),
            pltpu.VMEM((64, block, block), jnp.bfloat16),
            pltpu.SemaphoreType.DMA((6,)),
        ],
        compiler_params=pltpu.CompilerParams(vmem_limit_bytes=16 << 20),
    )(meta, plane_own.reshape(32, block, block), plane_far.reshape(32, block, block), a, b, ca, cb)[None]


def solution(mesh):
    fine = Mesh(mesh.devices.reshape(SIZES), AXES)
    wide, narrow = ("za", "zb", "core"), ("y", "x", "zh")
    return jax.shard_map(
        body,
        mesh=fine,
        in_specs=(
            P(wide, narrow, None, None),
            P(wide, narrow, None, None),
            P(wide, narrow, None, None),
            P(wide, narrow, None, None),
            P(wide, narrow, None),
            P(wide, narrow),
        ),
        out_specs=P(wide, narrow, None, None),
        check_vma=False,
    )
```

time: 598 us -> 136 us (0.23)
  the two profiles are of different devices: /device:TPU:1 before, /device:TPU:6 now
where the time goes in v1:
time: 136 us; the launch traced here: 135 us
  starting transfers between devices  74 us (54%)
  waiting for transfers between devices  47.2 us (35%)
  Pallas kernels  7.33 us (5%)
  local copies, waits for them, and re-layouts  6.03 us (4%)
    ppermute x8, starting transfers between devices, swap(): return lax.ppermute(value, axis, [(i, i ^ bits) for i in range(size)])  50.1 us
    ppermute x8, waiting for transfers between devices, swap(): return lax.ppermute(value, axis, [(i, i ^ bits) for i in range(size)])  42.2 us
    all_to_all x2, starting transfers between devices, gather_plane(): lax.all_to_all(spread, ('y', 'x'), split_axis=0, concat_axis=0, tiled=True)  23.9 us
    pallas_call x1, Pallas kernels, body(): pl.pallas_call(stacks_kernel, out_shape=jax.ShapeDtypeStruct((CSLOT, bloc...  7.33 us
    all_to_all x2, waiting for transfers between devices, gather_plane(): lax.all_to_all(spread, ('y', 'x'), split_axis=0, concat_axis=0, tiled=True)  5.04 us
    broadcast_in_dim x2, local copies, waits for them, and re-layouts, gather_plane(): spread = jnp.broadcast_to(value[None], (16,) + value.shape)  3.26 us
  transfers between devices with their start and end apart: 10, of which 4 were waited for; matrix products, arithmetic and copies ran while one was open for 2% of the time, Pallas kernels for 0%

profile of v1, /device:TPU:6, one launch (start us, length us, event | category | flops | bytes accessed | tf_op | source)
XLA Modules:
  0.0 135.5 jit_solution(6749918752961282473)
XLA Ops:
  0.0 2.0 %broadcast_in_dim.17 = bf16[16,2,128,128]{3,2,1,0:T(8,128)(2,1)} broadcast(bf16[2,128,128]{2,1,0:T(8,128)(2,1)} %bitcast.21), dimensions={1,2,3} | broadcast | bytes 1114112 | tf_op jit(solution)/shard_map/broadcast_in_dim | solution.py:21
  2.1 16.7 %all-to-all-start = ((bf16[16,2,128,128]{3,2,1,0:T(8,128)(2,1)}), bf16[16,2,128,128]{3,2,1,0:T(8,128)(2,1)S(1)}, u32[]{:S(2)}, u32[]{:S(2)}) async-start(bf16[16,2,128,128]{3,2,1,0:T(8,128)(2,1)} %broadcast_in_dim.17), calls=%async_computation | async-start | bytes 2097152 | tf_op jit(solution)/shard_map/all_to_all | solution.py:22
  18.8 6.6 %collective-permute-start.1 = (bf16[2,128,128]{2,1,0:T(8,128)(2,1)S(1)}, bf16[2,128,128]{2,1,0:T(8,128)(2,1)S(1)}, u32[]{:S(2)}, u32[]{:S(2)}) collective-permute-start(bf16[2,128,128]{2,1,0:T(8,128)(2,1)S(1)} %bitcast.18), channel_id=1, source_target_pairs={{0,512},{256,768},{512,0},{768,256},{1,513},{257,769},{513,1},{769... | collective-permute-start | bytes 196616 | tf_op jit(solution)/shard_map/ppermute | solution.py:17
  25.3 13.2 %collective-permute-done.1 = bf16[2,128,128]{2,1,0:T(8,128)(2,1)S(1)} collective-permute-done((bf16[2,128,128]{2,1,0:T(8,128)(2,1)S(1)}, bf16[2,128,128]{2,1,0:T(8,128)(2,1)S(1)}, u32[]{:S(2)}, u32[]{:S(2)}) %collective-permute-start.1) | collective-permute-done | bytes 65568 | tf_op jit(solution)/shard_map/ppermute | solution.py:17
  38.6 0.0 copy-start.1
  38.6 2.5 %collective-permute-start.2 = (bf16[4,128,128]{2,1,0:T(8,128)(2,1)S(1)}, bf16[4,128,128]{2,1,0:T(8,128)(2,1)S(1)}, u32[]{:S(2)}, u32[]{:S(2)}) collective-permute-start(bf16[4,128,128]{2,1,0:T(8,128)(2,1)S(1)} %pad_maximum_fusion.1), channel_id=1, source_target_pairs={{0,256},{256,0},{512,768},{768,512},{1,257},{257,1},{513,769},{769... | collective-permute-start | bytes 393224 | tf_op jit(solution)/shard_map/ppermute | solution.py:17
  41.1 11.3 %collective-permute-done.2 = bf16[4,128,128]{2,1,0:T(8,128)(2,1)S(1)} collective-permute-done((bf16[4,128,128]{2,1,0:T(8,128)(2,1)S(1)}, bf16[4,128,128]{2,1,0:T(8,128)(2,1)S(1)}, u32[]{:S(2)}, u32[]{:S(2)}) %collective-permute-start.2) | collective-permute-done | bytes 131104 | tf_op jit(solution)/shard_map/ppermute | solution.py:17
  52.4 1.9 %collective-permute-start.3 = (bf16[8,128,128]{2,1,0:T(8,128)(2,1)S(1)}, bf16[8,128,128]{2,1,0:T(8,128)(2,1)S(1)}, u32[]{:S(2)}, u32[]{:S(2)}) collective-permute-start(bf16[8,128,128]{2,1,0:T(8,128)(2,1)S(1)} %pad_maximum_fusion.a_h), channel_id=1, source_target_pairs={{0,64},{64,0},{128,192},{192,128},{1,65},{65,1},{129,193},{193,129... | collective-permute-start | bytes 786440 | tf_op jit(solution)/shard_map/ppermute | solution.py:17
  54.3 4.0 %collective-permute-start.4 = (bf16[8,128,128]{2,1,0:T(8,128)(2,1)S(1)}, bf16[8,128,128]{2,1,0:T(8,128)(2,1)}, u32[]{:S(2)}, u32[]{:S(2)}) collective-permute-start(bf16[8,128,128]{2,1,0:T(8,128)(2,1)S(1)} %pad_maximum_fusion.a_h), channel_id=1, source_target_pairs={{0,128},{64,192},{128,0},{192,64},{1,129},{65,193},{129,1},{193,65... | collective-permute-start | bytes 786440 | tf_op jit(solution)/shard_map/ppermute | solution.py:17
  58.3 4.2 %collective-permute-start.5 = (bf16[8,128,128]{2,1,0:T(8,128)(2,1)S(1)}, bf16[8,128,128]{2,1,0:T(8,128)(2,1)S(1)}, u32[]{:S(2)}, u32[]{:S(2)}) collective-permute-start(bf16[8,128,128]{2,1,0:T(8,128)(2,1)S(1)} %pad_maximum_fusion.a_h), channel_id=1, source_target_pairs={{0,192},{64,128},{128,64},{192,0},{1,193},{65,129},{129,65},{193,1... | collective-permute-start | bytes 786440 | tf_op jit(solution)/shard_map/ppermute | solution.py:17
  62.5 26.6 %collective-permute-start = (bf16[2,128,128]{2,1,0:T(8,128)(2,1)S(1)}, bf16[2,128,128]{2,1,0:T(8,128)(2,1)S(1)}, u32[]{:S(2)}, u32[]{:S(2)}) collective-permute-start(bf16[2,128,128]{2,1,0:T(8,128)(2,1)S(1)} %bitcast.22), channel_id=1, source_target_pairs={{0,1},{1,0},{2,3},{3,2},{4,5},{5,4},{6,7},{7,6},{8,9},{9,8},{10,11... | collective-permute-start | bytes 196616 | tf_op jit(solution)/shard_map/ppermute | solution.py:17
  89.2 0.0 collective-permute-done.3
  89.2 17.7 %collective-permute-done = bf16[2,128,128]{2,1,0:T(8,128)(2,1)S(1)} collective-permute-done((bf16[2,128,128]{2,1,0:T(8,128)(2,1)S(1)}, bf16[2,128,128]{2,1,0:T(8,128)(2,1)S(1)}, u32[]{:S(2)}, u32[]{:S(2)}) %collective-permute-start) | collective-permute-done | bytes 65568 | tf_op jit(solution)/shard_map/ppermute | solution.py:17
  106.9 0.0 all-to-all-done
  106.9 1.2 broadcast_in_dim.18
  108.1 7.2 %all-to-all-start.1 = ((bf16[16,2,128,128]{3,2,1,0:T(8,128)(2,1)}), bf16[16,2,128,128]{3,2,1,0:T(8,128)(2,1)S(1)}, u32[]{:S(2)}, u32[]{:S(2)}) async-start(bf16[16,2,128,128]{3,2,1,0:T(8,128)(2,1)} %broadcast_in_dim.18), calls=%async_computation.1 | async-start | bytes 2097152 | tf_op jit(solution)/shard_map/all_to_all | solution.py:22
  115.3 1.0 constant_dynamic-update-slice_fusion.1
  116.3 0.0 collective-permute-done.5
  116.3 0.0 copy-start.2
  116.4 1.9 %collective-permute-start.7 = (bf16[24,128,128]{2,1,0:T(8,128)(2,1)S(1)}, bf16[24,128,128]{2,1,0:T(8,128)(2,1)}, u32[]{:S(2)}, u32[]{:S(2)}) collective-permute-start(bf16[24,128,128]{2,1,0:T(8,128)(2,1)S(1)} %constant_dynamic-update-slice_fusion.b_h), channel_id=1, source_target_pairs={{0,32},{32,0},{1,33},{33,1},{2,34},{34,2},{3,35},{35,3},{4,36},{36... | collective-permute-start | bytes 2359304 | tf_op jit(solution)/shard_map/ppermute | solution.py:17
  118.3 2.4 %collective-permute-start.6 = (bf16[8,128,128]{2,1,0:T(8,128)(2,1)S(1)}, bf16[8,128,128]{2,1,0:T(8,128)(2,1)S(1)}, u32[]{:S(2)}, u32[]{:S(2)}) collective-permute-start(bf16[8,128,128]{2,1,0:T(8,128)(2,1)S(1)} %pad_maximum_fusion.a_h), channel_id=1, source_target_pairs={{0,32},{32,0},{1,33},{33,1},{2,34},{34,2},{3,35},{35,3},{4,36},{36... | collective-permute-start | bytes 786440 | tf_op jit(solution)/shard_map/ppermute | solution.py:17
  120.7 0.1 copy.7
  120.8 0.1 reshape.19
  120.9 0.6 copy-done.3
  121.5 0.1 copy.8
  121.6 0.1 reshape.20
  122.4 0.0 copy-start.4
  122.4 0.6 copy-done.4
  123.0 0.1 concatenate.13.meta
  123.1 5.0 %all-to-all-done.1 = bf16[16,2,128,128]{3,2,1,0:T(8,128)(2,1)S(1)} async-done(((bf16[16,2,128,128]{3,2,1,0:T(8,128)(2,1)}), bf16[16,2,128,128]{3,2,1,0:T(8,128)(2,1)S(1)}, u32[]{:S(2)}, u32[]{:S(2)}) %all-to-all-start.1) | async-done | bytes 1048608 | tf_op jit(solution)/shard_map/all_to_all | solution.py:22
  128.2 0.0 collective-permute-done.7.cb_h
  128.2 7.3 %shard_map.64 = f32[8,128,128]{2,1,0:T(8,128)} custom-call(s32[581]{0:T(1024)S(1)} %concatenate.13.meta, bf16[32,128,128]{2,1,0:T(8,128)(2,1)S(1)} %bitcast.16, bf16[32,128,128]{2,1,0:T(8,128)(2,1)S(1)} %bitcast.17, bf16[8,128,128]{2,1,0:T(8,128)(2,1)S(1)} %pad_maximum_fusion.a_h, bf16[24,128,128]{2,1,0:T(8,128)(2,1)S(1)} %constant_dynamic-update-slice_fusion.b_h, ...), custom_call_target="tpu_custom_call" | custom-call | tf_op jit(solution)/shard_map/pallas_call | solution.py:111
  (11 shorter events, 0.1 us)
Async XLA Ops:
  2.1 16.7 %copy-start = (bf16[2,1,128,128]{3,2,1,0:T(8,128)(2,1)S(1)}, bf16[2,1,128,128]{3,2,1,0:T(8,128)(2,1)}, u32[]{:S(2)}) copy-start(bf16[2,1,128,128]{3,2,1,0:T(8,128)(2,1)} %param.7) | copy-start | bytes 196612
  2.1 104.8 %all-to-all-start = ((bf16[16,2,128,128]{3,2,1,0:T(8,128)(2,1)}), bf16[16,2,128,128]{3,2,1,0:T(8,128)(2,1)S(1)}, u32[]{:S(2)}, u32[]{:S(2)}) async-start(bf16[16,2,128,128]{3,2,1,0:T(8,128)(2,1)} %broadcast_in_dim.17), calls=%async_computation | async-start | bytes 2097152 | tf_op jit(solution)/shard_map/all_to_all | solution.py:22
  18.8 19.8 %collective-permute-start.1 = (bf16[2,128,128]{2,1,0:T(8,128)(2,1)S(1)}, bf16[2,128,128]{2,1,0:T(8,128)(2,1)S(1)}, u32[]{:S(2)}, u32[]{:S(2)}) collective-permute-start(bf16[2,128,128]{2,1,0:T(8,128)(2,1)S(1)} %bitcast.18), channel_id=1, source_target_pairs={{0,512},{256,768},{512,0},{768,256},{1,513},{257,769},{513,1},{769... | collective-permute-start | bytes 196616 | tf_op jit(solution)/shard_map/ppermute | solution.py:17
  38.6 23.9 %copy-start.1 = (bf16[1,2,128,128]{3,2,1,0:T(8,128)(2,1)S(1)}, bf16[1,2,128,128]{3,2,1,0:T(8,128)(2,1)}, u32[]{:S(2)}) copy-start(bf16[1,2,128,128]{3,2,1,0:T(8,128)(2,1)} %param.6) | copy-start | bytes 196612
  38.6 13.8 %collective-permute-start.2 = (bf16[4,128,128]{2,1,0:T(8,128)(2,1)S(1)}, bf16[4,128,128]{2,1,0:T(8,128)(2,1)S(1)}, u32[]{:S(2)}, u32[]{:S(2)}) collective-permute-start(bf16[4,128,128]{2,1,0:T(8,128)(2,1)S(1)} %pad_maximum_fusion.1), channel_id=1, source_target_pairs={{0,256},{256,0},{512,768},{768,512},{1,257},{257,1},{513,769},{769... | collective-permute-start | bytes 393224 | tf_op jit(solution)/shard_map/ppermute | solution.py:17
  52.4 36.8 %collective-permute-start.3 = (bf16[8,128,128]{2,1,0:T(8,128)(2,1)S(1)}, bf16[8,128,128]{2,1,0:T(8,128)(2,1)S(1)}, u32[]{:S(2)}, u32[]{:S(2)}) collective-permute-start(bf16[8,128,128]{2,1,0:T(8,128)(2,1)S(1)} %pad_maximum_fusion.a_h), channel_id=1, source_target_pairs={{0,64},{64,0},{128,192},{192,128},{1,65},{65,1},{129,193},{193,129... | collective-permute-start | bytes 786440 | tf_op jit(solution)/shard_map/ppermute | solution.py:17
  54.3 61.0 %collective-permute-start.4 = (bf16[8,128,128]{2,1,0:T(8,128)(2,1)S(1)}, bf16[8,128,128]{2,1,0:T(8,128)(2,1)}, u32[]{:S(2)}, u32[]{:S(2)}) collective-permute-start(bf16[8,128,128]{2,1,0:T(8,128)(2,1)S(1)} %pad_maximum_fusion.a_h), channel_id=1, source_target_pairs={{0,128},{64,192},{128,0},{192,64},{1,129},{65,193},{129,1},{193,65... | collective-permute-start | bytes 786440 | tf_op jit(solution)/shard_map/ppermute | solution.py:17
  58.3 58.0 %collective-permute-start.5 = (bf16[8,128,128]{2,1,0:T(8,128)(2,1)S(1)}, bf16[8,128,128]{2,1,0:T(8,128)(2,1)S(1)}, u32[]{:S(2)}, u32[]{:S(2)}) collective-permute-start(bf16[8,128,128]{2,1,0:T(8,128)(2,1)S(1)} %pad_maximum_fusion.a_h), channel_id=1, source_target_pairs={{0,192},{64,128},{128,64},{192,0},{1,193},{65,129},{129,65},{193,1... | collective-permute-start | bytes 786440 | tf_op jit(solution)/shard_map/ppermute | solution.py:17
  62.5 44.3 %collective-permute-start = (bf16[2,128,128]{2,1,0:T(8,128)(2,1)S(1)}, bf16[2,128,128]{2,1,0:T(8,128)(2,1)S(1)}, u32[]{:S(2)}, u32[]{:S(2)}) collective-permute-start(bf16[2,128,128]{2,1,0:T(8,128)(2,1)S(1)} %bitcast.22), channel_id=1, source_target_pairs={{0,1},{1,0},{2,3},{3,2},{4,5},{5,4},{6,7},{7,6},{8,9},{9,8},{10,11... | collective-permute-start | bytes 196616 | tf_op jit(solution)/shard_map/ppermute | solution.py:17
  108.1 20.1 %all-to-all-start.1 = ((bf16[16,2,128,128]{3,2,1,0:T(8,128)(2,1)}), bf16[16,2,128,128]{3,2,1,0:T(8,128)(2,1)S(1)}, u32[]{:S(2)}, u32[]{:S(2)}) async-start(bf16[16,2,128,128]{3,2,1,0:T(8,128)(2,1)} %broadcast_in_dim.18), calls=%async_computation.1 | async-start | bytes 2097152 | tf_op jit(solution)/shard_map/all_to_all | solution.py:22
  116.3 4.4 %copy-start.2 = (s32[1,1,64,4]{2,3,1,0:T(4,128)S(1)}, s32[1,1,64,4]{2,3,1,0:T(4,128)}, u32[]{:S(2)}) copy-start(s32[1,1,64,4]{2,3,1,0:T(4,128)} %param.8) | copy-start | bytes 3076
  116.4 11.8 %collective-permute-start.7 = (bf16[24,128,128]{2,1,0:T(8,128)(2,1)S(1)}, bf16[24,128,128]{2,1,0:T(8,128)(2,1)}, u32[]{:S(2)}, u32[]{:S(2)}) collective-permute-start(bf16[24,128,128]{2,1,0:T(8,128)(2,1)S(1)} %constant_dynamic-update-slice_fusion.b_h), channel_id=1, source_target_pairs={{0,32},{32,0},{1,33},{33,1},{2,34},{34,2},{3,35},{35,3},{4,36},{36... | collective-permute-start | bytes 2359304 | tf_op jit(solution)/shard_map/ppermute | solution.py:17
  118.3 4.8 %collective-permute-start.6 = (bf16[8,128,128]{2,1,0:T(8,128)(2,1)S(1)}, bf16[8,128,128]{2,1,0:T(8,128)(2,1)S(1)}, u32[]{:S(2)}, u32[]{:S(2)}) collective-permute-start(bf16[8,128,128]{2,1,0:T(8,128)(2,1)S(1)} %pad_maximum_fusion.a_h), channel_id=1, source_target_pairs={{0,32},{32,0},{1,33},{33,1},{2,34},{34,2},{3,35},{35,3},{4,36},{36... | collective-permute-start | bytes 786440 | tf_op jit(solution)/shard_map/ppermute | solution.py:17
  120.8 0.7 copy-start.3
  122.4 0.7 copy-start.4

commit v2 on v1

--- a/solution.py
+++ b/solution.py
@@ -22,19 +22,12 @@
     return lax.all_to_all(spread, ("y", "x"), split_axis=0, concat_axis=0, tiled=True)
 
 
-def stacks_kernel(meta, own_h, far_h, a_h, b_h, ca_h, cb_h, out, left, right, sems):
-    copies = [
-        pltpu.make_async_copy(src, dst, sems.at[i])
-        for i, (src, dst) in enumerate(
-            (
-                (own_h, left.at[pl.ds(0, 32)]),
-                (far_h, left.at[pl.ds(32, 32)]),
-                (a_h, right.at[pl.ds(0, 8)]),
-                (b_h, right.at[pl.ds(8, 24)]),
-                (ca_h, right.at[pl.ds(32, 8)]),
-                (cb_h, right.at[pl.ds(40, 24)]),
-            )
-        )
+def stacks_kernel(meta, left_h, *refs):
+    pieces, (out, left, right, sems) = refs[:8], refs[8:]
+    copies = [pltpu.make_async_copy(left_h, left, sems.at[8])]
+    copies += [
+        pltpu.make_async_copy(piece, right.at[pl.ds(8 * i, 8)], sems.at[i])
+        for i, piece in enumerate(pieces)
     ]
     for copy in copies:
         copy.start()
@@ -43,8 +36,7 @@
     count = meta[576]
 
     def left_at(slot):
-        place = ((slot >> 2) << 1) + (slot & 1)
-        return place + ((((slot >> 1) & 1) ^ half) << 5)
+        return slot ^ (half << 1)
 
     def right_at(slot):
         far = (slot >> 4) ^ za
@@ -99,28 +91,27 @@
     )
     right_8 = swap(own_right, "za", Z_HI, 2)
     far_left = swap(own_left, "zh", 2, 1)
+    right_8, far_left = lax.optimization_barrier((right_8, far_left))
     pair = jnp.concatenate([own_right, right_8], 0)
     right_4 = swap(pair, "za", Z_HI, 1)
-    plane_own = gather_plane(own_left)
+    plane = gather_plane(jnp.concatenate([own_left, far_left], 0))
     a = jnp.concatenate([pair, right_4], 0)
-    b = jnp.concatenate([swap(a, "zb", Z_LO, k) for k in (1, 2, 3)], 0)
-    plane_far = gather_plane(far_left)
-    ca = swap(a, "core", 2, 1)
-    cb = swap(b, "core", 2, 1)
+    near = [a] + [swap(a, "zb", Z_LO, k) for k in (1, 2, 3)]
+    pieces = near + [swap(piece, "core", 2, 1) for piece in near]
     block = own_left.shape[1]
     return pl.pallas_call(
         stacks_kernel,
         out_shape=jax.ShapeDtypeStruct((CSLOT, block, block), jnp.float32),
         in_specs=[pl.BlockSpec(memory_space=pltpu.SMEM)]
-        + [pl.BlockSpec(memory_space=pl.ANY)] * 6,
+        + [pl.BlockSpec(memory_space=pl.ANY)] * 9,
         out_specs=pl.BlockSpec(memory_space=pltpu.VMEM),
         scratch_shapes=[
             pltpu.VMEM((64, block, block), jnp.bfloat16),
             pltpu.VMEM((64, block, block), jnp.bfloat16),
-            pltpu.SemaphoreType.DMA((6,)),
+            pltpu.SemaphoreType.DMA((9,)),
         ],
         compiler_params=pltpu.CompilerParams(vmem_limit_bytes=16 << 20),
-    )(meta, plane_own.reshape(32, block, block), plane_far.reshape(32, block, block), a, b, ca, cb)[None]
+    )(meta, plane.reshape(64, block, block), *pieces)[None]
 
 
 def solution(mesh):

time: 136 us -> 114 us (0.84)
  the two profiles are of different devices: /device:TPU:6 before, /device:TPU:25 now
where the time goes in v2:
time: 114 us
  starting transfers between devices  95.7 us (84%)
  waiting for transfers between devices  7.35 us (6%)
  Pallas kernels  6.42 us (6%)
  local copies, waits for them, and re-layouts  2.34 us (2%)
    ppermute x10, starting transfers between devices, swap(): return lax.ppermute(value, axis, [(i, i ^ bits) for i in range(size)])  89 us
    ppermute x10, waiting for transfers between devices, swap(): return lax.ppermute(value, axis, [(i, i ^ bits) for i in range(size)])  7.35 us
    all_to_all x1, starting transfers between devices, gather_plane(): lax.all_to_all(spread, ('y', 'x'), split_axis=0, concat_axis=0, tiled=True)  6.75 us
    pallas_call x1, Pallas kernels, body(): pl.pallas_call(stacks_kernel, out_shape=jax.ShapeDtypeStruct((CSLOT, bloc...  6.42 us
  transfers between devices with their start and end apart: 11, of which 3 were waited for; matrix products, arithmetic and copies ran while one was open for 0% of the time, Pallas kernels for 0%

profile of v2, /device:TPU:25, one launch (start us, length us, event | category | flops | bytes accessed | tf_op | source)
XLA Modules:
  0.0 113.6 jit_solution(1161614960836709147)
XLA Ops:
  0.0 15.4 %collective-permute-start = (bf16[2,128,128]{2,1,0:T(8,128)(2,1)}, bf16[2,128,128]{2,1,0:T(8,128)(2,1)S(1)}, u32[]{:S(2)}, u32[]{:S(2)}) collective-permute-start(bf16[2,128,128]{2,1,0:T(8,128)(2,1)} %bitcast.16), channel_id=1, source_target_pairs={{0,512},{256,768},{512,0},{768,256},{1,513},{257,769},{513,1},{769... | collective-permute-start | bytes 196616 | tf_op jit(solution)/shard_map/ppermute | solution.py:17
  15.4 19.1 %collective-permute-start.1 = (bf16[2,128,128]{2,1,0:T(8,128)(2,1)}, bf16[2,128,128]{2,1,0:T(8,128)(2,1)S(1)}, u32[]{:S(2)}, u32[]{:S(2)}) collective-permute-start(bf16[2,128,128]{2,1,0:T(8,128)(2,1)} %bitcast.19), channel_id=1, source_target_pairs={{0,1},{1,0},{2,3},{3,2},{4,5},{5,4},{6,7},{7,6},{8,9},{9,8},{10,11... | collective-permute-start | bytes 196616 | tf_op jit(solution)/shard_map/ppermute | solution.py:17
  34.5 0.0 collective-permute-done
  34.5 4.6 %collective-permute-done.1 = bf16[2,128,128]{2,1,0:T(8,128)(2,1)S(1)} collective-permute-done((bf16[2,128,128]{2,1,0:T(8,128)(2,1)}, bf16[2,128,128]{2,1,0:T(8,128)(2,1)S(1)}, u32[]{:S(2)}, u32[]{:S(2)}) %collective-permute-start.1) | collective-permute-done | bytes 65568 | tf_op jit(solution)/shard_map/ppermute | solution.py:17
  39.1 0.9 pad_maximum_fusion.1
  40.0 1.8 %broadcast_in_dim.4 = bf16[16,4,128,128]{3,2,1,0:T(8,128)(2,1)} broadcast(bf16[4,128,128]{2,1,0:T(8,128)(2,1)S(1)} %pad_maximum_fusion.1), dimensions={1,2,3} | broadcast | bytes 2228224 | tf_op jit(solution)/shard_map/broadcast_in_dim | solution.py:21
  41.8 6.8 %all-to-all-start = ((bf16[16,4,128,128]{3,2,1,0:T(8,128)(2,1)}), bf16[16,4,128,128]{3,2,1,0:T(8,128)(2,1)S(1)}, u32[]{:S(2)}, u32[]{:S(2)}) async-start(bf16[16,4,128,128]{3,2,1,0:T(8,128)(2,1)} %broadcast_in_dim.4), calls=%async_computation | async-start | bytes 4194304 | tf_op jit(solution)/shard_map/all_to_all | solution.py:22
  48.6 0.0 copy-done
  48.6 10.7 %collective-permute-start.2 = (bf16[4,128,128]{2,1,0:T(8,128)(2,1)S(1)}, bf16[4,128,128]{2,1,0:T(8,128)(2,1)S(1)}, u32[]{:S(2)}, u32[]{:S(2)}) collective-permute-start(bf16[4,128,128]{2,1,0:T(8,128)(2,1)S(1)} %pad_maximum_fusion.2), channel_id=1, source_target_pairs={{0,256},{256,0},{512,768},{768,512},{1,257},{257,1},{513,769},{769... | collective-permute-start | bytes 393224 | tf_op jit(solution)/shard_map/ppermute | solution.py:17
  59.3 2.3 %collective-permute-done.2 = bf16[4,128,128]{2,1,0:T(8,128)(2,1)S(1)} collective-permute-done((bf16[4,128,128]{2,1,0:T(8,128)(2,1)S(1)}, bf16[4,128,128]{2,1,0:T(8,128)(2,1)S(1)}, u32[]{:S(2)}, u32[]{:S(2)}) %collective-permute-start.2) | collective-permute-done | bytes 131104 | tf_op jit(solution)/shard_map/ppermute | solution.py:17
  61.7 12.8 %collective-permute-start.3 = (bf16[8,128,128]{2,1,0:T(8,128)(2,1)S(1)}, bf16[8,128,128]{2,1,0:T(8,128)(2,1)S(1)}, u32[]{:S(2)}, u32[]{:S(2)}) collective-permute-start(bf16[8,128,128]{2,1,0:T(8,128)(2,1)S(1)} %pad_maximum_fusion.refs_0_), channel_id=1, source_target_pairs={{0,64},{64,0},{128,192},{192,128},{1,65},{65,1},{129,193},{193,129... | collective-permute-start | bytes 786440 | tf_op jit(solution)/shard_map/ppermute | solution.py:17
  74.4 6.0 %collective-permute-start.4 = (bf16[8,128,128]{2,1,0:T(8,128)(2,1)S(1)}, bf16[8,128,128]{2,1,0:T(8,128)(2,1)S(1)}, u32[]{:S(2)}, u32[]{:S(2)}) collective-permute-start(bf16[8,128,128]{2,1,0:T(8,128)(2,1)S(1)} %pad_maximum_fusion.refs_0_), channel_id=1, source_target_pairs={{0,128},{64,192},{128,0},{192,64},{1,129},{65,193},{129,1},{193,65... | collective-permute-start | bytes 786440 | tf_op jit(solution)/shard_map/ppermute | solution.py:17
  80.4 1.9 %collective-permute-start.5 = (bf16[8,128,128]{2,1,0:T(8,128)(2,1)S(1)}, bf16[8,128,128]{2,1,0:T(8,128)(2,1)S(1)}, u32[]{:S(2)}, u32[]{:S(2)}) collective-permute-start(bf16[8,128,128]{2,1,0:T(8,128)(2,1)S(1)} %pad_maximum_fusion.refs_0_), channel_id=1, source_target_pairs={{0,192},{64,128},{128,64},{192,0},{1,193},{65,129},{129,65},{193,1... | collective-permute-start | bytes 786440 | tf_op jit(solution)/shard_map/ppermute | solution.py:17
  82.3 6.8 %collective-permute-start.6 = (bf16[8,128,128]{2,1,0:T(8,128)(2,1)S(1)}, bf16[8,128,128]{2,1,0:T(8,128)(2,1)S(1)}, u32[]{:S(2)}, u32[]{:S(2)}) collective-permute-start(bf16[8,128,128]{2,1,0:T(8,128)(2,1)S(1)} %pad_maximum_fusion.refs_0_), channel_id=1, source_target_pairs={{0,32},{32,0},{1,33},{33,1},{2,34},{34,2},{3,35},{35,3},{4,36},{36... | collective-permute-start | bytes 786440 | tf_op jit(solution)/shard_map/ppermute | solution.py:17
  89.1 0.0 collective-permute-done.3.refs_1_
  89.1 1.9 %collective-permute-start.7 = (bf16[8,128,128]{2,1,0:T(8,128)(2,1)S(1)}, bf16[8,128,128]{2,1,0:T(8,128)(2,1)}, u32[]{:S(2)}, u32[]{:S(2)}) collective-permute-start(bf16[8,128,128]{2,1,0:T(8,128)(2,1)S(1)} %collective-permute-done.3.refs_1_), channel_id=1, source_target_pairs={{0,32},{32,0},{1,33},{33,1},{2,34},{34,2},{3,35},{35,3},{4,36},{36... | collective-permute-start | bytes 786440 | tf_op jit(solution)/shard_map/ppermute | solution.py:17
  91.0 0.0 collective-permute-done.4.refs_2_
  91.1 12.5 %collective-permute-start.8 = (bf16[8,128,128]{2,1,0:T(8,128)(2,1)S(1)}, bf16[8,128,128]{2,1,0:T(8,128)(2,1)}, u32[]{:S(2)}, u32[]{:S(2)}) collective-permute-start(bf16[8,128,128]{2,1,0:T(8,128)(2,1)S(1)} %collective-permute-done.4.refs_2_), channel_id=1, source_target_pairs={{0,32},{32,0},{1,33},{33,1},{2,34},{34,2},{3,35},{35,3},{4,36},{36... | collective-permute-start | bytes 786440 | tf_op jit(solution)/shard_map/ppermute | solution.py:17
  103.6 0.0 collective-permute-done.5.refs_3_
  103.6 1.9 %collective-permute-start.9 = (bf16[8,128,128]{2,1,0:T(8,128)(2,1)S(1)}, bf16[8,128,128]{2,1,0:T(8,128)(2,1)}, u32[]{:S(2)}, u32[]{:S(2)}) collective-permute-start(bf16[8,128,128]{2,1,0:T(8,128)(2,1)S(1)} %collective-permute-done.5.refs_3_), channel_id=1, source_target_pairs={{0,32},{32,0},{1,33},{33,1},{2,34},{34,2},{3,35},{35,3},{4,36},{36... | collective-permute-start | bytes 786440 | tf_op jit(solution)/shard_map/ppermute | solution.py:17
  105.5 0.1 copy.7
  105.6 0.1 reshape.16
  105.7 0.0 copy-done.2
  105.8 0.1 copy.8
  105.9 0.1 reshape.17
  106.6 0.1 concatenate.13.meta
  106.7 0.0 collective-permute-done.6.refs_4_
  106.7 0.0 collective-permute-done.7.refs_5_
  106.7 0.0 collective-permute-done.8.refs_6_
  106.7 0.4 collective-permute-done.9.refs_7_
  107.2 0.0 all-to-all-done
  107.2 6.4 %shard_map.64 = f32[8,128,128]{2,1,0:T(8,128)} custom-call(s32[581]{0:T(1024)S(1)} %concatenate.13.meta, bf16[64,128,128]{2,1,0:T(8,128)(2,1)S(1)} %bitcast.15, bf16[8,128,128]{2,1,0:T(8,128)(2,1)S(1)} %pad_maximum_fusion.refs_0_, bf16[8,128,128]{2,1,0:T(8,128)(2,1)S(1)} %collective-permute-done.3.refs_1_, ...), custom_call_target="tpu_custom_call" | custom-call | tf_op jit(solution)/shard_map/pallas_call | solution.py:102
  (8 shorter events, 0.1 us)
Async XLA Ops:
  0.0 34.5 %collective-permute-start = (bf16[2,128,128]{2,1,0:T(8,128)(2,1)}, bf16[2,128,128]{2,1,0:T(8,128)(2,1)S(1)}, u32[]{:S(2)}, u32[]{:S(2)}) collective-permute-start(bf16[2,128,128]{2,1,0:T(8,128)(2,1)} %bitcast.16), channel_id=1, source_target_pairs={{0,512},{256,768},{512,0},{768,256},{1,513},{257,769},{513,1},{769... | collective-permute-start | bytes 196616 | tf_op jit(solution)/shard_map/ppermute | solution.py:17
  15.4 23.7 %collective-permute-start.1 = (bf16[2,128,128]{2,1,0:T(8,128)(2,1)}, bf16[2,128,128]{2,1,0:T(8,128)(2,1)S(1)}, u32[]{:S(2)}, u32[]{:S(2)}) collective-permute-start(bf16[2,128,128]{2,1,0:T(8,128)(2,1)} %bitcast.19), channel_id=1, source_target_pairs={{0,1},{1,0},{2,3},{3,2},{4,5},{5,4},{6,7},{7,6},{8,9},{9,8},{10,11... | collective-permute-start | bytes 196616 | tf_op jit(solution)/shard_map/ppermute | solution.py:17
  41.8 6.8 %copy-start = (bf16[2,1,128,128]{3,2,1,0:T(8,128)(2,1)S(1)}, bf16[2,1,128,128]{3,2,1,0:T(8,128)(2,1)}, u32[]{:S(2)}) copy-start(bf16[2,1,128,128]{3,2,1,0:T(8,128)(2,1)} %param.7) | copy-start | bytes 196612
  41.8 63.7 %copy-start.1 = (s32[1,1,64,4]{2,3,1,0:T(4,128)S(1)}, s32[1,1,64,4]{2,3,1,0:T(4,128)}, u32[]{:S(2)}) copy-start(s32[1,1,64,4]{2,3,1,0:T(4,128)} %param.8) | copy-start | bytes 3076
  41.8 63.9 %copy-start.2 = (s32[1,1,64,4]{2,3,1,0:T(4,128)S(1)}, s32[1,1,64,4]{2,3,1,0:T(4,128)}, u32[]{:S(2)}) copy-start(s32[1,1,64,4]{2,3,1,0:T(4,128)} %param.9) | copy-start | bytes 3076
  41.8 64.8 %copy-start.3 = (s32[1,1,64]{2,1,0:T(1,128)S(1)}, s32[1,1,64]{2,1,0:T(1,128)}, u32[]{:S(2)}) copy-start(s32[1,1,64]{2,1,0:T(1,128)} %param.10) | copy-start | bytes 772
  41.8 65.4 %all-to-all-start = ((bf16[16,4,128,128]{3,2,1,0:T(8,128)(2,1)}), bf16[16,4,128,128]{3,2,1,0:T(8,128)(2,1)S(1)}, u32[]{:S(2)}, u32[]{:S(2)}) async-start(bf16[16,4,128,128]{3,2,1,0:T(8,128)(2,1)} %broadcast_in_dim.4), calls=%async_computation | async-start | bytes 4194304 | tf_op jit(solution)/shard_map/all_to_all | solution.py:22
  48.6 13.0 %collective-permute-start.2 = (bf16[4,128,128]{2,1,0:T(8,128)(2,1)S(1)}, bf16[4,128,128]{2,1,0:T(8,128)(2,1)S(1)}, u32[]{:S(2)}, u32[]{:S(2)}) collective-permute-start(bf16[4,128,128]{2,1,0:T(8,128)(2,1)S(1)} %pad_maximum_fusion.2), channel_id=1, source_target_pairs={{0,256},{256,0},{512,768},{768,512},{1,257},{257,1},{513,769},{769... | collective-permute-start | bytes 393224 | tf_op jit(solution)/shard_map/ppermute | solution.py:17
  61.7 27.5 %collective-permute-start.3 = (bf16[8,128,128]{2,1,0:T(8,128)(2,1)S(1)}, bf16[8,128,128]{2,1,0:T(8,128)(2,1)S(1)}, u32[]{:S(2)}, u32[]{:S(2)}) collective-permute-start(bf16[8,128,128]{2,1,0:T(8,128)(2,1)S(1)} %pad_maximum_fusion.refs_0_), channel_id=1, source_target_pairs={{0,64},{64,0},{128,192},{192,128},{1,65},{65,1},{129,193},{193,129... | collective-permute-start | bytes 786440 | tf_op jit(solution)/shard_map/ppermute | solution.py:17
  74.4 16.6 %collective-permute-start.4 = (bf16[8,128,128]{2,1,0:T(8,128)(2,1)S(1)}, bf16[8,128,128]{2,1,0:T(8,128)(2,1)S(1)}, u32[]{:S(2)}, u32[]{:S(2)}) collective-permute-start(bf16[8,128,128]{2,1,0:T(8,128)(2,1)S(1)} %pad_maximum_fusion.refs_0_), channel_id=1, source_target_pairs={{0,128},{64,192},{128,0},{192,64},{1,129},{65,193},{129,1},{193,65... | collective-permute-start | bytes 786440 | tf_op jit(solution)/shard_map/ppermute | solution.py:17
  80.4 23.2 %collective-permute-start.5 = (bf16[8,128,128]{2,1,0:T(8,128)(2,1)S(1)}, bf16[8,128,128]{2,1,0:T(8,128)(2,1)S(1)}, u32[]{:S(2)}, u32[]{:S(2)}) collective-permute-start(bf16[8,128,128]{2,1,0:T(8,128)(2,1)S(1)} %pad_maximum_fusion.refs_0_), channel_id=1, source_target_pairs={{0,192},{64,128},{128,64},{192,0},{1,193},{65,129},{129,65},{193,1... | collective-permute-start | bytes 786440 | tf_op jit(solution)/shard_map/ppermute | solution.py:17
  82.3 24.4 %collective-permute-start.6 = (bf16[8,128,128]{2,1,0:T(8,128)(2,1)S(1)}, bf16[8,128,128]{2,1,0:T(8,128)(2,1)S(1)}, u32[]{:S(2)}, u32[]{:S(2)}) collective-permute-start(bf16[8,128,128]{2,1,0:T(8,128)(2,1)S(1)} %pad_maximum_fusion.refs_0_), channel_id=1, source_target_pairs={{0,32},{32,0},{1,33},{33,1},{2,34},{34,2},{3,35},{35,3},{4,36},{36... | collective-permute-start | bytes 786440 | tf_op jit(solution)/shard_map/ppermute | solution.py:17
  89.1 17.6 %collective-permute-start.7 = (bf16[8,128,128]{2,1,0:T(8,128)(2,1)S(1)}, bf16[8,128,128]{2,1,0:T(8,128)(2,1)}, u32[]{:S(2)}, u32[]{:S(2)}) collective-permute-start(bf16[8,128,128]{2,1,0:T(8,128)(2,1)S(1)} %collective-permute-done.3.refs_1_), channel_id=1, source_target_pairs={{0,32},{32,0},{1,33},{33,1},{2,34},{34,2},{3,35},{35,3},{4,36},{36... | collective-permute-start | bytes 786440 | tf_op jit(solution)/shard_map/ppermute | solution.py:17
  91.1 15.7 %collective-permute-start.8 = (bf16[8,128,128]{2,1,0:T(8,128)(2,1)S(1)}, bf16[8,128,128]{2,1,0:T(8,128)(2,1)}, u32[]{:S(2)}, u32[]{:S(2)}) collective-permute-start(bf16[8,128,128]{2,1,0:T(8,128)(2,1)S(1)} %collective-permute-done.4.refs_2_), channel_id=1, source_target_pairs={{0,32},{32,0},{1,33},{33,1},{2,34},{34,2},{3,35},{35,3},{4,36},{36... | collective-permute-start | bytes 786440 | tf_op jit(solution)/shard_map/ppermute | solution.py:17
  103.6 3.6 %collective-permute-start.9 = (bf16[8,128,128]{2,1,0:T(8,128)(2,1)S(1)}, bf16[8,128,128]{2,1,0:T(8,128)(2,1)}, u32[]{:S(2)}, u32[]{:S(2)}) collective-permute-start(bf16[8,128,128]{2,1,0:T(8,128)(2,1)S(1)} %collective-permute-done.5.refs_3_), channel_id=1, source_target_pairs={{0,32},{32,0},{1,33},{33,1},{2,34},{34,2},{3,35},{35,3},{4,36},{36... | collective-permute-start | bytes 786440 | tf_op jit(solution)/shard_map/ppermute | solution.py:17

commit v3 on v2

v3 whole, which is shorter than its diff:
```python
import jax
import jax.numpy as jnp
from jax import lax
from jax.experimental import pallas as pl
from jax.experimental.pallas import tpu as pltpu
from jax.sharding import Mesh
from jax.sharding import PartitionSpec as P

CSLOT = 8
UNROLL = 8
Z_HI, Z_LO = 4, 4
AXES = ("za", "zb", "core", "y", "x", "zh")
SIZES = (Z_HI, Z_LO, 2, 4, 4, 2)
LONG = 10**11


def swap(value, axis, size, bits):
    return lax.ppermute(value, axis, [(i, i ^ bits) for i in range(size)])


def gather_plane(value):
    spread = jnp.broadcast_to(value[None], (16,) + value.shape)
    return lax.all_to_all(spread, ("y", "x"), split_axis=0, concat_axis=0, tiled=True)


def hold(value, name):
    def kernel(ref, same):
        pass

    return pl.pallas_call(
        kernel,
        out_shape=jax.ShapeDtypeStruct(value.shape, value.dtype),
        in_specs=[pl.BlockSpec(memory_space=pl.ANY)],
        out_specs=pl.BlockSpec(memory_space=pl.ANY),
        input_output_aliases={0: 0},
        cost_estimate=pl.CostEstimate(flops=LONG, bytes_accessed=0, transcendentals=0),
        name=name,
    )(value)


def stacks_kernel(lefts_at, rights_at, slots, counts, left, *refs):
    pieces, (out, right) = refs[:-2], refs[-2:]
    first = 0
    for piece in pieces:
        right[pl.ds(first, piece.shape[0])] = piece[...]
        first += piece.shape[0]
    out[...] = jnp.zeros_like(out)
    za, zb, core, half = (lax.axis_index(a) for a in ("za", "zb", "core", "zh"))
    count = counts[0, 0]

    def left_at(slot):
        return slot ^ (half << 1)

    def right_at(slot):
        far = (slot >> 4) ^ za
        near = ((slot >> 2) & 3) ^ zb
        other = ((slot >> 1) & 1) ^ core
        return (other << 5) + ((far & 1) << 4) + (near << 2) + (far & 2) + (slot & 1)

    def stack_sum(t):
        lefts = [left[left_at(lefts_at[g, t])] for g in range(4)]
        rights = [right[right_at(rights_at[g, t])] for g in range(4)]
        return jnp.dot(
            jnp.concatenate(lefts, 1),
            jnp.concatenate(rights, 0),
            preferred_element_type=jnp.float32,
        )

    def step(i, carry):
        first = i * UNROLL
        sums = [stack_sum(first + u) for u in range(UNROLL)]
        for u in range(UNROLL):
            slot = slots[first + u]
            out[slot] = out[slot] + jnp.where(first + u < count, sums[u], 0.0)
        return carry

    lax.fori_loop(0, lax.div(count + UNROLL - 1, UNROLL), step, 0)


def body(left_values, right_values, stack_left, stack_right, stack_slot, stack_count):
    own_left = left_values[0]
    own_right = right_values[:, 0]
    right_8 = swap(own_right, "za", Z_HI, 2)
    far_left = swap(own_left, "zh", 2, 1)
    pair = hold(jnp.concatenate([own_right, right_8], 0), "pair")
    right_4 = swap(pair, "za", Z_HI, 1)
    early = [swap(pair, "zb", Z_LO, k) for k in (1, 2, 3)]
    rest = hold(right_4, "rest")
    plane = gather_plane(jnp.concatenate([own_left, far_left], 0))
    late = [swap(rest, "zb", Z_LO, k) for k in (1, 2, 3)]
    early = jnp.concatenate([pair] + early, 0)
    late = jnp.concatenate([rest] + late, 0)
    pieces = [early, late]
    pieces += [swap(piece, "core", 2, 1) for piece in pieces]
    block = own_left.shape[1]
    return pl.pallas_call(
        stacks_kernel,
        out_shape=jax.ShapeDtypeStruct((CSLOT, block, block), jnp.float32),
        in_specs=[pl.BlockSpec(memory_space=pltpu.SMEM)] * 4
        + [pl.BlockSpec(memory_space=pltpu.VMEM)] * (1 + len(pieces)),
        out_specs=pl.BlockSpec(memory_space=pltpu.VMEM),
        scratch_shapes=[pltpu.VMEM((64, block, block), jnp.bfloat16)],
        compiler_params=pltpu.CompilerParams(vmem_limit_bytes=32 << 20),
    )(
        stack_left[0, 0].T,
        stack_right[0, 0].T,
        stack_slot[0, 0],
        stack_count,
        plane.reshape(64, block, block),
        *pieces,
    )[None]


def solution(mesh):
    fine = Mesh(mesh.devices.reshape(SIZES), AXES)
    wide, narrow = ("za", "zb", "core"), ("y", "x", "zh")
    return jax.shard_map(
        body,
        mesh=fine,
        in_specs=(
            P(wide, narrow, None, None),
            P(wide, narrow, None, None),
            P(wide, narrow, None, None),
            P(wide, narrow, None, None),
            P(wide, narrow, None),
            P(wide, narrow),
        ),
        out_specs=P(wide, narrow, None, None),
        check_vma=False,
    )
```

time: 114 us -> 96.9 us (0.85)
  the two profiles are of different devices: /device:TPU:25 before, /device:TPU:233 now
where the time goes in v3:
time: 96.9 us; the launch traced here: 96.3 us
  starting transfers between devices  65.4 us (67%)
  waiting for transfers between devices  16 us (17%)
  local copies, waits for them, and re-layouts  6.15 us (6%)
  Pallas kernels  5.23 us (5%)
  other arithmetic  2.56 us (3%)
    ppermute x11, starting transfers between devices, swap(): return lax.ppermute(value, axis, [(i, i ^ bits) for i in range(size)])  58.6 us
    ppermute x11, waiting for transfers between devices, swap(): return lax.ppermute(value, axis, [(i, i ^ bits) for i in range(size)])  9.27 us
    all_to_all x1, starting transfers between devices, gather_plane(): lax.all_to_all(spread, ('y', 'x'), split_axis=0, concat_axis=0, tiled=True)  6.83 us
    all_to_all x1, waiting for transfers between devices, gather_plane(): lax.all_to_all(spread, ('y', 'x'), split_axis=0, concat_axis=0, tiled=True)  6.76 us
    pallas_call x1, Pallas kernels, body(): pl.pallas_call(stacks_kernel, out_shape=jax.ShapeDtypeStruct((CSLOT, bloc...  5.23 us
    unnamed x20, local copies, waits for them, and re-layouts  4.32 us
  transfers between devices with their start and end apart: 12, of which 4 were waited for; matrix products, arithmetic and copies ran while one was open for 5% of the time, Pallas kernels for 0%

profile of v3, /device:TPU:233, one launch (start us, length us, event | category | flops | bytes accessed | tf_op | source)
XLA Modules:
  0.0 96.3 jit_solution(438829614123667524)
XLA Ops:
  0.0 15.4 %collective-permute-start.1 = (bf16[2,128,128]{2,1,0:T(8,128)(2,1)}, bf16[2,128,128]{2,1,0:T(8,128)(2,1)S(1)}, u32[]{:S(2)}, u32[]{:S(2)}) collective-permute-start(bf16[2,128,128]{2,1,0:T(8,128)(2,1)} %bitcast.15), channel_id=1, source_target_pairs={{0,512},{256,768},{512,0},{768,256},{1,513},{257,769},{513,1},{769... | collective-permute-start | bytes 196616 | tf_op jit(solution)/shard_map/ppermute | solution.py:18
  15.4 11.6 %collective-permute-start = (bf16[2,128,128]{2,1,0:T(8,128)(2,1)}, bf16[2,128,128]{2,1,0:T(8,128)(2,1)S(1)}, u32[]{:S(2)}, u32[]{:S(2)}) collective-permute-start(bf16[2,128,128]{2,1,0:T(8,128)(2,1)} %bitcast.17), channel_id=1, source_target_pairs={{0,1},{1,0},{2,3},{3,2},{4,5},{5,4},{6,7},{7,6},{8,9},{9,8},{10,11... | collective-permute-start | bytes 196616 | tf_op jit(solution)/shard_map/ppermute | solution.py:18
  27.0 0.0 collective-permute-done.1
  27.0 1.5 %pad_maximum_fusion.3.ref = bf16[4,128,128]{2,1,0:T(8,128)(2,1)} fusion(bf16[2,128,128]{2,1,0:T(8,128)(2,1)S(1)} %collective-permute-done.1, bf16[2,128,128]{2,1,0:T(8,128)(2,1)} %bitcast.16), kind=kLoop, calls=%fused_computation.3 | loop fusion | flops 65536 | bytes 262144 | tf_op jit(solution)/shard_map/concatenate | solution.py:85
  28.5 5.3 %collective-permute-start.5 = (bf16[4,128,128]{2,1,0:T(8,128)(2,1)}, bf16[4,128,128]{2,1,0:T(8,128)(2,1)S(1)}, u32[]{:S(2)}, u32[]{:S(2)}) collective-permute-start(bf16[4,128,128]{2,1,0:T(8,128)(2,1)} %pair.1), channel_id=1, source_target_pairs={{0,256},{256,0},{512,768},{768,512},{1,257},{257,1},{513,769},{769... | collective-permute-start | bytes 393224 | tf_op jit(solution)/shard_map/ppermute | solution.py:18
  33.9 3.5 %collective-permute-start.4 = (bf16[4,128,128]{2,1,0:T(8,128)(2,1)}, bf16[4,128,128]{2,1,0:T(8,128)(2,1)S(1)}, u32[]{:S(2)}, u32[]{:S(2)}) collective-permute-start(bf16[4,128,128]{2,1,0:T(8,128)(2,1)} %pair.1), channel_id=1, source_target_pairs={{0,192},{64,128},{128,64},{192,0},{1,193},{65,129},{129,65},{193,1... | collective-permute-start | bytes 393224 | tf_op jit(solution)/shard_map/ppermute | solution.py:18
  37.4 2.2 %collective-permute-start.3 = (bf16[4,128,128]{2,1,0:T(8,128)(2,1)}, bf16[4,128,128]{2,1,0:T(8,128)(2,1)S(1)}, u32[]{:S(2)}, u32[]{:S(2)}) collective-permute-start(bf16[4,128,128]{2,1,0:T(8,128)(2,1)} %pair.1), channel_id=1, source_target_pairs={{0,128},{64,192},{128,0},{192,64},{1,129},{65,193},{129,1},{193,65... | collective-permute-start | bytes 393224 | tf_op jit(solution)/shard_map/ppermute | solution.py:18
  39.6 3.5 %collective-permute-start.2 = (bf16[4,128,128]{2,1,0:T(8,128)(2,1)}, bf16[4,128,128]{2,1,0:T(8,128)(2,1)S(1)}, u32[]{:S(2)}, u32[]{:S(2)}) collective-permute-start(bf16[4,128,128]{2,1,0:T(8,128)(2,1)} %pair.1), channel_id=1, source_target_pairs={{0,64},{64,0},{128,192},{192,128},{1,65},{65,1},{129,193},{193,129... | collective-permute-start | bytes 393224 | tf_op jit(solution)/shard_map/ppermute | solution.py:18
  43.1 7.7 %collective-permute-done = bf16[2,128,128]{2,1,0:T(8,128)(2,1)S(1)} collective-permute-done((bf16[2,128,128]{2,1,0:T(8,128)(2,1)}, bf16[2,128,128]{2,1,0:T(8,128)(2,1)S(1)}, u32[]{:S(2)}, u32[]{:S(2)}) %collective-permute-start) | collective-permute-done | bytes 65568 | tf_op jit(solution)/shard_map/ppermute | solution.py:18
  50.9 1.8 %broadcast_in_dim.4 = bf16[16,4,128,128]{3,2,1,0:T(8,128)(2,1)} broadcast(bf16[4,128,128]{2,1,0:T(8,128)(2,1)S(1)} %pad_maximum_fusion.2), dimensions={1,2,3} | broadcast | bytes 2228224 | tf_op jit(solution)/shard_map/broadcast_in_dim | solution.py:22
  52.7 6.8 %all-to-all-start = ((bf16[16,4,128,128]{3,2,1,0:T(8,128)(2,1)}), bf16[16,4,128,128]{3,2,1,0:T(8,128)(2,1)S(1)}, u32[]{:S(2)}, u32[]{:S(2)}) async-start(bf16[16,4,128,128]{3,2,1,0:T(8,128)(2,1)} %broadcast_in_dim.4), calls=%async_computation | async-start | bytes 4194304 | tf_op jit(solution)/shard_map/all_to_all | solution.py:23
  59.6 0.6 copy-done.8
  60.2 2.0 %collective-permute-start.8 = (bf16[4,128,128]{2,1,0:T(8,128)(2,1)}, bf16[4,128,128]{2,1,0:T(8,128)(2,1)S(1)}, u32[]{:S(2)}, u32[]{:S(2)}) collective-permute-start(bf16[4,128,128]{2,1,0:T(8,128)(2,1)} %rest.1), channel_id=1, source_target_pairs={{0,192},{64,128},{128,64},{192,0},{1,193},{65,129},{129,65},{193,1... | collective-permute-start | bytes 393224 | tf_op jit(solution)/shard_map/ppermute | solution.py:18
  62.3 1.9 %collective-permute-start.7 = (bf16[4,128,128]{2,1,0:T(8,128)(2,1)}, bf16[4,128,128]{2,1,0:T(8,128)(2,1)S(1)}, u32[]{:S(2)}, u32[]{:S(2)}) collective-permute-start(bf16[4,128,128]{2,1,0:T(8,128)(2,1)} %rest.1), channel_id=1, source_target_pairs={{0,128},{64,192},{128,0},{192,64},{1,129},{65,193},{129,1},{193,65... | collective-permute-start | bytes 393224 | tf_op jit(solution)/shard_map/ppermute | solution.py:18
  64.2 0.0 collective-permute-done.4
  64.2 5.4 %collective-permute-start.6 = (bf16[4,128,128]{2,1,0:T(8,128)(2,1)}, bf16[4,128,128]{2,1,0:T(8,128)(2,1)S(1)}, u32[]{:S(2)}, u32[]{:S(2)}) collective-permute-start(bf16[4,128,128]{2,1,0:T(8,128)(2,1)} %rest.1), channel_id=1, source_target_pairs={{0,64},{64,0},{128,192},{192,128},{1,65},{65,1},{129,193},{193,129... | collective-permute-start | bytes 393224 | tf_op jit(solution)/shard_map/ppermute | solution.py:18
  69.7 0.0 collective-permute-done.2
  69.7 0.1 pad_maximum_fusion.refs_0_
  69.8 4.0 %collective-permute-start.9 = (bf16[16,128,128]{2,1,0:T(8,128)(2,1)S(1)}, bf16[16,128,128]{2,1,0:T(8,128)(2,1)S(1)}, u32[]{:S(2)}, u32[]{:S(2)}) collective-permute-start(bf16[16,128,128]{2,1,0:T(8,128)(2,1)S(1)} %pad_maximum_fusion.refs_0_), channel_id=1, source_target_pairs={{0,32},{32,0},{1,33},{33,1},{2,34},{34,2},{3,35},{35,3},{4,36},{36... | collective-permute-start | bytes 1572872 | tf_op jit(solution)/shard_map/ppermute | solution.py:18
  73.8 0.0 collective-permute-done.8
  73.8 1.5 %collective-permute-done.7 = bf16[4,128,128]{2,1,0:T(8,128)(2,1)S(1)} collective-permute-done((bf16[4,128,128]{2,1,0:T(8,128)(2,1)}, bf16[4,128,128]{2,1,0:T(8,128)(2,1)S(1)}, u32[]{:S(2)}, u32[]{:S(2)}) %collective-permute-start.7) | collective-permute-done | bytes 131104 | tf_op jit(solution)/shard_map/ppermute | solution.py:18
  75.3 0.0 collective-permute-done.6
  75.3 1.0 %pad_maximum_fusion.1.refs_1_ = bf16[16,128,128]{2,1,0:T(8,128)(2,1)S(1)} fusion(bf16[4,128,128]{2,1,0:T(8,128)(2,1)S(1)} %collective-permute-done.8, bf16[4,128,128]{2,1,0:T(8,128)(2,1)S(1)} %collective-permute-done.7, bf16[4,128,128]{2,1,0:T(8,128)(2,1)S(1)} %collective-permute-done.6, bf16[4,128,128]{2,1,0:T(8,128)(2,1)} %rest.1), kind=kLoop, calls=%fused_computation.1 | loop fusion | flops 786432 | bytes 1048576 | tf_op jit(solution)/shard_map/concatenate | solution.py:92
  76.3 3.6 %collective-permute-start.10 = (bf16[16,128,128]{2,1,0:T(8,128)(2,1)S(1)}, bf16[16,128,128]{2,1,0:T(8,128)(2,1)S(1)}, u32[]{:S(2)}, u32[]{:S(2)}) collective-permute-start(bf16[16,128,128]{2,1,0:T(8,128)(2,1)S(1)} %pad_maximum_fusion.1.refs_1_), channel_id=1, source_target_pairs={{0,32},{32,0},{1,33},{33,1},{2,34},{34,2},{3,35},{35,3},{4,36},{36... | collective-permute-start | bytes 1572872 | tf_op jit(solution)/shard_map/ppermute | solution.py:18
  80.5 0.0 copy-start
  80.5 0.8 copy-done
  81.3 0.1 collective-permute-done.10.refs_3_
  81.4 0.8 copy-done.2
  82.2 6.8 %all-to-all-done = bf16[16,4,128,128]{3,2,1,0:T(8,128)(2,1)S(1)} async-done(((bf16[16,4,128,128]{3,2,1,0:T(8,128)(2,1)}), bf16[16,4,128,128]{3,2,1,0:T(8,128)(2,1)S(1)}, u32[]{:S(2)}, u32[]{:S(2)}) %all-to-all-start) | async-done | bytes 2097184 | tf_op jit(solution)/shard_map/all_to_all | solution.py:23
  89.0 1.0 %copy-done.1 = bf16[16,128,128]{2,1,0:T(8,128)(2,1)S(1)} copy-done((bf16[16,128,128]{2,1,0:T(8,128)(2,1)S(1)}, bf16[16,128,128]{2,1,0:T(8,128)(2,1)}, u32[]{:S(2)}) %copy-start.1) | copy-done | bytes 524312
  90.0 1.0 %copy-done.3 = bf16[16,128,128]{2,1,0:T(8,128)(2,1)S(1)} copy-done((bf16[16,128,128]{2,1,0:T(8,128)(2,1)S(1)}, bf16[16,128,128]{2,1,0:T(8,128)(2,1)}, u32[]{:S(2)}) %copy-start.3) | copy-done | bytes 524312
  91.0 5.2 %shard_map.64 = f32[8,128,128]{2,1,0:T(8,128)} custom-call(s32[4,64]{1,0:T(4,128)S(1)} %bitcast.12, s32[4,64]{1,0:T(4,128)S(1)} %bitcast.13, s32[64]{0:T(128)S(1)} %bitcast.14, s32[1,1]{1,0:T(1,128)S(6)} %copy.11.counts, bf16[64,128,128]{2,1,0:T(8,128)(2,1)S(1)} %bitcast.11, bf16[16,128,128]{2,1,0:T(8,128)(2,1)S(1)} %pad_maximum_fusion.refs_0_, ...), custom_call_target="tpu_custom_call" | custom-call | tf_op jit(solution)/shard_map/pallas_call | solution.py:96
  (20 shorter events, 0.0 us)
Async XLA Ops:
  0.0 27.0 %collective-permute-start.1 = (bf16[2,128,128]{2,1,0:T(8,128)(2,1)}, bf16[2,128,128]{2,1,0:T(8,128)(2,1)S(1)}, u32[]{:S(2)}, u32[]{:S(2)}) collective-permute-start(bf16[2,128,128]{2,1,0:T(8,128)(2,1)} %bitcast.15), channel_id=1, source_target_pairs={{0,512},{256,768},{512,0},{768,256},{1,513},{257,769},{513,1},{769... | collective-permute-start | bytes 196616 | tf_op jit(solution)/shard_map/ppermute | solution.py:18
  15.4 35.4 %collective-permute-start = (bf16[2,128,128]{2,1,0:T(8,128)(2,1)}, bf16[2,128,128]{2,1,0:T(8,128)(2,1)S(1)}, u32[]{:S(2)}, u32[]{:S(2)}) collective-permute-start(bf16[2,128,128]{2,1,0:T(8,128)(2,1)} %bitcast.17), channel_id=1, source_target_pairs={{0,1},{1,0},{2,3},{3,2},{4,5},{5,4},{6,7},{7,6},{8,9},{9,8},{10,11... | collective-permute-start | bytes 196616 | tf_op jit(solution)/shard_map/ppermute | solution.py:18
  28.5 22.3 %copy-start.9 = (bf16[1,2,128,128]{3,2,1,0:T(8,128)(2,1)S(1)}, bf16[1,2,128,128]{3,2,1,0:T(8,128)(2,1)}, u32[]{:S(2)}) copy-start(bf16[1,2,128,128]{3,2,1,0:T(8,128)(2,1)} %param.6) | copy-start | bytes 196612
  28.5 31.0 %collective-permute-start.5 = (bf16[4,128,128]{2,1,0:T(8,128)(2,1)}, bf16[4,128,128]{2,1,0:T(8,128)(2,1)S(1)}, u32[]{:S(2)}, u32[]{:S(2)}) collective-permute-start(bf16[4,128,128]{2,1,0:T(8,128)(2,1)} %pair.1), channel_id=1, source_target_pairs={{0,256},{256,0},{512,768},{768,512},{1,257},{257,1},{513,769},{769... | collective-permute-start | bytes 393224 | tf_op jit(solution)/shard_map/ppermute | solution.py:18
  33.9 30.4 %collective-permute-start.4 = (bf16[4,128,128]{2,1,0:T(8,128)(2,1)}, bf16[4,128,128]{2,1,0:T(8,128)(2,1)S(1)}, u32[]{:S(2)}, u32[]{:S(2)}) collective-permute-start(bf16[4,128,128]{2,1,0:T(8,128)(2,1)} %pair.1), channel_id=1, source_target_pairs={{0,192},{64,128},{128,64},{192,0},{1,193},{65,129},{129,65},{193,1... | collective-permute-start | bytes 393224 | tf_op jit(solution)/shard_map/ppermute | solution.py:18
  37.4 32.3 %collective-permute-start.3 = (bf16[4,128,128]{2,1,0:T(8,128)(2,1)}, bf16[4,128,128]{2,1,0:T(8,128)(2,1)S(1)}, u32[]{:S(2)}, u32[]{:S(2)}) collective-permute-start(bf16[4,128,128]{2,1,0:T(8,128)(2,1)} %pair.1), channel_id=1, source_target_pairs={{0,128},{64,192},{128,0},{192,64},{1,129},{65,193},{129,1},{193,65... | collective-permute-start | bytes 393224 | tf_op jit(solution)/shard_map/ppermute | solution.py:18
  39.6 30.1 %collective-permute-start.2 = (bf16[4,128,128]{2,1,0:T(8,128)(2,1)}, bf16[4,128,128]{2,1,0:T(8,128)(2,1)S(1)}, u32[]{:S(2)}, u32[]{:S(2)}) collective-permute-start(bf16[4,128,128]{2,1,0:T(8,128)(2,1)} %pair.1), channel_id=1, source_target_pairs={{0,64},{64,0},{128,192},{192,128},{1,65},{65,1},{129,193},{193,129... | collective-permute-start | bytes 393224 | tf_op jit(solution)/shard_map/ppermute | solution.py:18
  52.7 36.2 %all-to-all-start = ((bf16[16,4,128,128]{3,2,1,0:T(8,128)(2,1)}), bf16[16,4,128,128]{3,2,1,0:T(8,128)(2,1)S(1)}, u32[]{:S(2)}, u32[]{:S(2)}) async-start(bf16[16,4,128,128]{3,2,1,0:T(8,128)(2,1)} %broadcast_in_dim.4), calls=%async_computation | async-start | bytes 4194304 | tf_op jit(solution)/shard_map/all_to_all | solution.py:23
  59.5 10.1 %copy-start.7 = (bf16[4,128,128]{2,1,0:T(8,128)(2,1)S(1)}, bf16[4,128,128]{2,1,0:T(8,128)(2,1)}, u32[]{:S(2)}) copy-start(bf16[4,128,128]{2,1,0:T(8,128)(2,1)} %pair.1) | copy-start | bytes 393220
  59.6 0.7 copy-start.8
  60.2 28.7 %copy-start.4 = (s32[1,1,64,4]{2,3,1,0:T(4,128)S(1)}, s32[1,1,64,4]{2,3,1,0:T(4,128)}, u32[]{:S(2)}) copy-start(s32[1,1,64,4]{2,3,1,0:T(4,128)} %param.8) | copy-start | bytes 3076
  60.2 28.7 %copy-start.5 = (s32[1,1,64,4]{2,3,1,0:T(4,128)S(1)}, s32[1,1,64,4]{2,3,1,0:T(4,128)}, u32[]{:S(2)}) copy-start(s32[1,1,64,4]{2,3,1,0:T(4,128)} %param.9) | copy-start | bytes 3076
  60.2 28.7 %copy-start.6 = (s32[1,1,64]{2,1,0:T(1,128)S(1)}, s32[1,1,64]{2,1,0:T(1,128)}, u32[]{:S(2)}) copy-start(s32[1,1,64]{2,1,0:T(1,128)} %param.10) | copy-start | bytes 772
  60.2 13.6 %collective-permute-start.8 = (bf16[4,128,128]{2,1,0:T(8,128)(2,1)}, bf16[4,128,128]{2,1,0:T(8,128)(2,1)S(1)}, u32[]{:S(2)}, u32[]{:S(2)}) collective-permute-start(bf16[4,128,128]{2,1,0:T(8,128)(2,1)} %rest.1), channel_id=1, source_target_pairs={{0,192},{64,128},{128,64},{192,0},{1,193},{65,129},{129,65},{193,1... | collective-permute-start | bytes 393224 | tf_op jit(solution)/shard_map/ppermute | solution.py:18
  62.3 13.0 %collective-permute-start.7 = (bf16[4,128,128]{2,1,0:T(8,128)(2,1)}, bf16[4,128,128]{2,1,0:T(8,128)(2,1)S(1)}, u32[]{:S(2)}, u32[]{:S(2)}) collective-permute-start(bf16[4,128,128]{2,1,0:T(8,128)(2,1)} %rest.1), channel_id=1, source_target_pairs={{0,128},{64,192},{128,0},{192,64},{1,129},{65,193},{129,1},{193,65... | collective-permute-start | bytes 393224 | tf_op jit(solution)/shard_map/ppermute | solution.py:18
  64.2 11.1 %collective-permute-start.6 = (bf16[4,128,128]{2,1,0:T(8,128)(2,1)}, bf16[4,128,128]{2,1,0:T(8,128)(2,1)S(1)}, u32[]{:S(2)}, u32[]{:S(2)}) collective-permute-start(bf16[4,128,128]{2,1,0:T(8,128)(2,1)} %rest.1), channel_id=1, source_target_pairs={{0,64},{64,0},{128,192},{192,128},{1,65},{65,1},{129,193},{193,129... | collective-permute-start | bytes 393224 | tf_op jit(solution)/shard_map/ppermute | solution.py:18
  69.8 10.8 %collective-permute-start.9 = (bf16[16,128,128]{2,1,0:T(8,128)(2,1)S(1)}, bf16[16,128,128]{2,1,0:T(8,128)(2,1)S(1)}, u32[]{:S(2)}, u32[]{:S(2)}) collective-permute-start(bf16[16,128,128]{2,1,0:T(8,128)(2,1)S(1)} %pad_maximum_fusion.refs_0_), channel_id=1, source_target_pairs={{0,32},{32,0},{1,33},{33,1},{2,34},{34,2},{3,35},{35,3},{4,36},{36... | collective-permute-start | bytes 1572872 | tf_op jit(solution)/shard_map/ppermute | solution.py:18
  76.3 5.1 %collective-permute-start.10 = (bf16[16,128,128]{2,1,0:T(8,128)(2,1)S(1)}, bf16[16,128,128]{2,1,0:T(8,128)(2,1)S(1)}, u32[]{:S(2)}, u32[]{:S(2)}) collective-permute-start(bf16[16,128,128]{2,1,0:T(8,128)(2,1)S(1)} %pad_maximum_fusion.1.refs_1_), channel_id=1, source_target_pairs={{0,32},{32,0},{1,33},{33,1},{2,34},{34,2},{3,35},{35,3},{4,36},{36... | collective-permute-start | bytes 1572872 | tf_op jit(solution)/shard_map/ppermute | solution.py:18
  80.5 0.8 copy-start
  81.4 0.8 copy-start.2
  89.0 1.0 %copy-start.1 = (bf16[16,128,128]{2,1,0:T(8,128)(2,1)S(1)}, bf16[16,128,128]{2,1,0:T(8,128)(2,1)}, u32[]{:S(2)}) copy-start(bf16[16,128,128]{2,1,0:T(8,128)(2,1)} %copy-done) | copy-start | bytes 1572868
  90.0 1.0 %copy-start.3 = (bf16[16,128,128]{2,1,0:T(8,128)(2,1)S(1)}, bf16[16,128,128]{2,1,0:T(8,128)(2,1)}, u32[]{:S(2)}) copy-start(bf16[16,128,128]{2,1,0:T(8,128)(2,1)} %copy-done.2) | copy-start | bytes 1572868

commit v4 on v3

--- a/solution.py
+++ b/solution.py
@@ -7,7 +7,7 @@
 from jax.sharding import PartitionSpec as P
 
 CSLOT = 8
-UNROLL = 8
+UNROLL = 16
 Z_HI, Z_LO = 4, 4
 AXES = ("za", "zb", "core", "y", "x", "zh")
 SIZES = (Z_HI, Z_LO, 2, 4, 4, 2)
@@ -18,30 +18,36 @@
     return lax.ppermute(value, axis, [(i, i ^ bits) for i in range(size)])
 
 
-def gather_plane(value):
-    spread = jnp.broadcast_to(value[None], (16,) + value.shape)
-    return lax.all_to_all(spread, ("y", "x"), split_axis=0, concat_axis=0, tiled=True)
+def exchange_plane(value):
+    return lax.all_to_all(value, ("y", "x"), split_axis=0, concat_axis=0, tiled=True)
 
 
-def hold(value, name):
+def hold(value, name, cost=0):
     def kernel(ref, same):
         pass
 
     return pl.pallas_call(
         kernel,
-        out_shape=jax.ShapeDtypeStruct(value.shape, value.dtype),
-        in_specs=[pl.BlockSpec(memory_space=pl.ANY)],
-        out_specs=pl.BlockSpec(memory_space=pl.ANY),
+        out_shape=pltpu.VMEM(value.shape, value.dtype),
+        in_specs=[pl.BlockSpec(memory_space=pltpu.VMEM)],
+        out_specs=pl.BlockSpec(memory_space=pltpu.VMEM),
         input_output_aliases={0: 0},
-        cost_estimate=pl.CostEstimate(flops=LONG, bytes_accessed=0, transcendentals=0),
+        cost_estimate=pl.CostEstimate(flops=cost, bytes_accessed=0, transcendentals=0),
         name=name,
     )(value)
 
 
 def stacks_kernel(lefts_at, rights_at, slots, counts, left, *refs):
-    pieces, (out, right) = refs[:-2], refs[-2:]
+    pieces, (out, right, sems) = refs[:-3], refs[-3:]
+    own, other = pieces[: len(pieces) // 2], pieces[len(pieces) // 2 :]
+    copies, first = [], 32
+    for i, piece in enumerate(other):
+        place = right.at[pl.ds(first, piece.shape[0])]
+        copies.append(pltpu.make_async_copy(piece, place, sems.at[i]))
+        copies[-1].start()
+        first += piece.shape[0]
     first = 0
-    for piece in pieces:
+    for piece in own:
         right[pl.ds(first, piece.shape[0])] = piece[...]
         first += piece.shape[0]
     out[...] = jnp.zeros_like(out)
@@ -66,6 +72,9 @@
             preferred_element_type=jnp.float32,
         )
 
+    for copy in copies:
+        copy.wait()
+
     def step(i, carry):
         first = i * UNROLL
         sums = [stack_sum(first + u) for u in range(UNROLL)]
@@ -82,25 +91,33 @@
     own_right = right_values[:, 0]
     right_8 = swap(own_right, "za", Z_HI, 2)
     far_left = swap(own_left, "zh", 2, 1)
-    pair = hold(jnp.concatenate([own_right, right_8], 0), "pair")
+    pair = hold(jnp.concatenate([own_right, right_8], 0), "pair", LONG)
     right_4 = swap(pair, "za", Z_HI, 1)
     early = [swap(pair, "zb", Z_LO, k) for k in (1, 2, 3)]
-    rest = hold(right_4, "rest")
-    plane = gather_plane(jnp.concatenate([own_left, far_left], 0))
+    rest = hold(right_4, "rest", LONG)
+    halves = jnp.concatenate([own_left, far_left], 0)
+    plane = exchange_plane(jnp.broadcast_to(halves[None], (16,) + halves.shape))
     late = [swap(rest, "zb", Z_LO, k) for k in (1, 2, 3)]
     early = jnp.concatenate([pair] + early, 0)
     late = jnp.concatenate([rest] + late, 0)
     pieces = [early, late]
-    pieces += [swap(piece, "core", 2, 1) for piece in pieces]
+    pieces += [
+        pltpu.with_memory_space_constraint(swap(piece, "core", 2, 1), pltpu.HBM)
+        for piece in pieces
+    ]
     block = own_left.shape[1]
     return pl.pallas_call(
         stacks_kernel,
         out_shape=jax.ShapeDtypeStruct((CSLOT, block, block), jnp.float32),
         in_specs=[pl.BlockSpec(memory_space=pltpu.SMEM)] * 4
-        + [pl.BlockSpec(memory_space=pltpu.VMEM)] * (1 + len(pieces)),
+        + [pl.BlockSpec(memory_space=pltpu.VMEM)] * (1 + len(pieces) // 2)
+        + [pl.BlockSpec(memory_space=pltpu.HBM)] * (len(pieces) // 2),
         out_specs=pl.BlockSpec(memory_space=pltpu.VMEM),
-        scratch_shapes=[pltpu.VMEM((64, block, block), jnp.bfloat16)],
-        compiler_params=pltpu.CompilerParams(vmem_limit_bytes=32 << 20),
+        scratch_shapes=[
+            pltpu.VMEM((64, block, block), jnp.bfloat16),
+            pltpu.SemaphoreType.DMA((len(pieces) // 2,)),
+        ],
+        compiler_params=pltpu.CompilerParams(vmem_limit_bytes=8 << 20),
     )(
         stack_left[0, 0].T,
         stack_right[0, 0].T,

time: 96.9 us -> 94.2 us (0.972)
  the two profiles are of different devices: /device:TPU:233 before, /device:TPU:160 now
where the time goes in v4:
time: 94.2 us; the launch traced here: 93.6 us
  starting transfers between devices  64.3 us (68%)
  waiting for transfers between devices  20.7 us (22%)
  Pallas kernels  4.12 us (4%)
  local copies, waits for them, and re-layouts  2.68 us (3%)
  other arithmetic  1.01 us (1%)
    ppermute x11, starting transfers between devices, swap(): return lax.ppermute(value, axis, [(i, i ^ bits) for i in range(size)])  57.2 us
    all_to_all x1, waiting for transfers between devices, exchange_plane(): lax.all_to_all(value, ('y', 'x'), split_axis=0, concat_axis=0, tiled=True)  10.7 us
    ppermute x11, waiting for transfers between devices, swap(): return lax.ppermute(value, axis, [(i, i ^ bits) for i in range(size)])  9.95 us
    all_to_all x1, starting transfers between devices, exchange_plane(): lax.all_to_all(value, ('y', 'x'), split_axis=0, concat_axis=0, tiled=True)  7.03 us
    pallas_call x1, Pallas kernels, body(): pl.pallas_call(stacks_kernel, out_shape=jax.ShapeDtypeStruct((CSLOT, bloc...  4.11 us
  transfers between devices with their start and end apart: 12, of which 6 were waited for; matrix products, arithmetic and copies ran while one was open for 3% of the time, Pallas kernels for 0%

profile of v4, /device:TPU:160, one launch (start us, length us, event | category | flops | bytes accessed | tf_op | source)
XLA Modules:
  0.0 93.6 jit_solution(7216847763508015186)
XLA Ops:
  0.0 15.7 %collective-permute-start.1 = (bf16[2,128,128]{2,1,0:T(8,128)(2,1)}, bf16[2,128,128]{2,1,0:T(8,128)(2,1)S(1)}, u32[]{:S(2)}, u32[]{:S(2)}) collective-permute-start(bf16[2,128,128]{2,1,0:T(8,128)(2,1)} %bitcast.15), channel_id=1, source_target_pairs={{0,512},{256,768},{512,0},{768,256},{1,513},{257,769},{513,1},{769... | collective-permute-start | bytes 196616 | tf_op jit(solution)/shard_map/ppermute | solution.py:18
  15.7 13.7 %collective-permute-start = (bf16[2,128,128]{2,1,0:T(8,128)(2,1)}, bf16[2,128,128]{2,1,0:T(8,128)(2,1)S(1)}, u32[]{:S(2)}, u32[]{:S(2)}) collective-permute-start(bf16[2,128,128]{2,1,0:T(8,128)(2,1)} %bitcast.17), channel_id=1, source_target_pairs={{0,1},{1,0},{2,3},{3,2},{4,5},{5,4},{6,7},{7,6},{8,9},{9,8},{10,11... | collective-permute-start | bytes 196616 | tf_op jit(solution)/shard_map/ppermute | solution.py:18
  29.4 0.0 collective-permute-done.1
  29.4 0.9 pad_maximum_fusion.3.ref
  30.3 0.0 copy-start.4
  30.3 5.5 %collective-permute-start.5 = (bf16[4,128,128]{2,1,0:T(8,128)(2,1)S(1)}, bf16[4,128,128]{2,1,0:T(8,128)(2,1)S(1)}, u32[]{:S(2)}, u32[]{:S(2)}) collective-permute-start(bf16[4,128,128]{2,1,0:T(8,128)(2,1)S(1)} %pair.1), channel_id=1, source_target_pairs={{0,256},{256,0},{512,768},{768,512},{1,257},{257,1},{513,769},{769... | collective-permute-start | bytes 393224 | tf_op jit(solution)/shard_map/ppermute | solution.py:18
  35.7 2.9 %collective-permute-start.4 = (bf16[4,128,128]{2,1,0:T(8,128)(2,1)S(1)}, bf16[4,128,128]{2,1,0:T(8,128)(2,1)S(1)}, u32[]{:S(2)}, u32[]{:S(2)}) collective-permute-start(bf16[4,128,128]{2,1,0:T(8,128)(2,1)S(1)} %pair.1), channel_id=1, source_target_pairs={{0,192},{64,128},{128,64},{192,0},{1,193},{65,129},{129,65},{193,1... | collective-permute-start | bytes 393224 | tf_op jit(solution)/shard_map/ppermute | solution.py:18
  38.7 4.3 %collective-permute-start.3 = (bf16[4,128,128]{2,1,0:T(8,128)(2,1)S(1)}, bf16[4,128,128]{2,1,0:T(8,128)(2,1)S(1)}, u32[]{:S(2)}, u32[]{:S(2)}) collective-permute-start(bf16[4,128,128]{2,1,0:T(8,128)(2,1)S(1)} %pair.1), channel_id=1, source_target_pairs={{0,128},{64,192},{128,0},{192,64},{1,129},{65,193},{129,1},{193,65... | collective-permute-start | bytes 393224 | tf_op jit(solution)/shard_map/ppermute | solution.py:18
  42.9 2.0 %collective-permute-start.2 = (bf16[4,128,128]{2,1,0:T(8,128)(2,1)S(1)}, bf16[4,128,128]{2,1,0:T(8,128)(2,1)S(1)}, u32[]{:S(2)}, u32[]{:S(2)}) collective-permute-start(bf16[4,128,128]{2,1,0:T(8,128)(2,1)S(1)} %pair.1), channel_id=1, source_target_pairs={{0,64},{64,0},{128,192},{192,128},{1,65},{65,1},{129,193},{193,129... | collective-permute-start | bytes 393224 | tf_op jit(solution)/shard_map/ppermute | solution.py:18
  45.0 7.0 %collective-permute-done = bf16[2,128,128]{2,1,0:T(8,128)(2,1)S(1)} collective-permute-done((bf16[2,128,128]{2,1,0:T(8,128)(2,1)}, bf16[2,128,128]{2,1,0:T(8,128)(2,1)S(1)}, u32[]{:S(2)}, u32[]{:S(2)}) %collective-permute-start) | collective-permute-done | bytes 65568 | tf_op jit(solution)/shard_map/ppermute | solution.py:18
  52.0 1.8 %broadcast_in_dim.4 = bf16[16,4,128,128]{3,2,1,0:T(8,128)(2,1)} broadcast(bf16[4,128,128]{2,1,0:T(8,128)(2,1)S(1)} %pad_maximum_fusion.2), dimensions={1,2,3} | broadcast | bytes 2228224 | tf_op jit(solution)/shard_map/broadcast_in_dim | solution.py:99
  53.9 7.0 %all-to-all-start = ((bf16[16,4,128,128]{3,2,1,0:T(8,128)(2,1)}), bf16[16,4,128,128]{3,2,1,0:T(8,128)(2,1)S(1)}, u32[]{:S(2)}, u32[]{:S(2)}) async-start(bf16[16,4,128,128]{3,2,1,0:T(8,128)(2,1)} %broadcast_in_dim.4), calls=%async_computation | async-start | bytes 4194304 | tf_op jit(solution)/shard_map/all_to_all | solution.py:22
  60.9 0.0 collective-permute-done.5.ref
  60.9 0.0 copy-start
  60.9 0.0 copy-start.1
  61.0 0.0 copy-start.2
  61.0 2.1 %collective-permute-start.8 = (bf16[4,128,128]{2,1,0:T(8,128)(2,1)S(1)}, bf16[4,128,128]{2,1,0:T(8,128)(2,1)S(1)}, u32[]{:S(2)}, u32[]{:S(2)}) collective-permute-start(bf16[4,128,128]{2,1,0:T(8,128)(2,1)S(1)} %rest.1), channel_id=1, source_target_pairs={{0,192},{64,128},{128,64},{192,0},{1,193},{65,129},{129,65},{193,1... | collective-permute-start | bytes 393224 | tf_op jit(solution)/shard_map/ppermute | solution.py:18
  63.0 3.9 %collective-permute-start.7 = (bf16[4,128,128]{2,1,0:T(8,128)(2,1)S(1)}, bf16[4,128,128]{2,1,0:T(8,128)(2,1)S(1)}, u32[]{:S(2)}, u32[]{:S(2)}) collective-permute-start(bf16[4,128,128]{2,1,0:T(8,128)(2,1)S(1)} %rest.1), channel_id=1, source_target_pairs={{0,128},{64,192},{128,0},{192,64},{1,129},{65,193},{129,1},{193,65... | collective-permute-start | bytes 393224 | tf_op jit(solution)/shard_map/ppermute | solution.py:18
  66.9 0.0 collective-permute-done.4
  66.9 3.4 %collective-permute-start.6 = (bf16[4,128,128]{2,1,0:T(8,128)(2,1)S(1)}, bf16[4,128,128]{2,1,0:T(8,128)(2,1)S(1)}, u32[]{:S(2)}, u32[]{:S(2)}) collective-permute-start(bf16[4,128,128]{2,1,0:T(8,128)(2,1)S(1)} %rest.1), channel_id=1, source_target_pairs={{0,64},{64,0},{128,192},{192,128},{1,65},{65,1},{129,193},{193,129... | collective-permute-start | bytes 393224 | tf_op jit(solution)/shard_map/ppermute | solution.py:18
  70.4 0.0 collective-permute-done.2
  70.4 0.1 pad_maximum_fusion.refs_0_
  70.4 1.9 %collective-permute-start.9 = (bf16[16,128,128]{2,1,0:T(8,128)(2,1)S(1)}, bf16[16,128,128]{2,1,0:T(8,128)(2,1)S(1)}, u32[]{:S(2)}, u32[]{:S(2)}) collective-permute-start(bf16[16,128,128]{2,1,0:T(8,128)(2,1)S(1)} %pad_maximum_fusion.refs_0_), channel_id=1, source_target_pairs={{0,32},{32,0},{1,33},{33,1},{2,34},{34,2},{3,35},{35,3},{4,36},{36... | collective-permute-start | bytes 1572872 | tf_op jit(solution)/shard_map/ppermute | solution.py:18
  72.4 1.0 %collective-permute-done.8 = bf16[4,128,128]{2,1,0:T(8,128)(2,1)S(1)} collective-permute-done((bf16[4,128,128]{2,1,0:T(8,128)(2,1)S(1)}, bf16[4,128,128]{2,1,0:T(8,128)(2,1)S(1)}, u32[]{:S(2)}, u32[]{:S(2)}) %collective-permute-start.8) | collective-permute-done | bytes 131104 | tf_op jit(solution)/shard_map/ppermute | solution.py:18
  73.4 0.5 collective-permute-done.7
  73.9 0.8 collective-permute-done.6
  74.8 0.1 pad_maximum_fusion.1.refs_1_
  74.8 1.9 %collective-permute-start.10 = (bf16[16,128,128]{2,1,0:T(8,128)(2,1)S(1)}, bf16[16,128,128]{2,1,0:T(8,128)(2,1)}, u32[]{:S(2)}, u32[]{:S(2)}) collective-permute-start(bf16[16,128,128]{2,1,0:T(8,128)(2,1)S(1)} %pad_maximum_fusion.1.refs_1_), channel_id=1, source_target_pairs={{0,32},{32,0},{1,33},{33,1},{2,34},{34,2},{3,35},{35,3},{4,36},{36... | collective-permute-start | bytes 1572872 | tf_op jit(solution)/shard_map/ppermute | solution.py:18
  77.4 0.8 copy-done.3
  78.2 0.5 collective-permute-done.10.refs_3_
  78.8 10.7 %all-to-all-done = bf16[16,4,128,128]{3,2,1,0:T(8,128)(2,1)S(1)} async-done(((bf16[16,4,128,128]{3,2,1,0:T(8,128)(2,1)}), bf16[16,4,128,128]{3,2,1,0:T(8,128)(2,1)S(1)}, u32[]{:S(2)}, u32[]{:S(2)}) %all-to-all-start) | async-done | bytes 2097184 | tf_op jit(solution)/shard_map/all_to_all | solution.py:22
  89.5 4.1 %shard_map.64 = f32[8,128,128]{2,1,0:T(8,128)} custom-call(s32[4,64]{1,0:T(4,128)S(1)} %bitcast.12, s32[4,64]{1,0:T(4,128)S(1)} %bitcast.13, s32[64]{0:T(128)S(1)} %bitcast.14, s32[1,1]{1,0:T(1,128)S(6)} %copy.11.counts, bf16[64,128,128]{2,1,0:T(8,128)(2,1)S(1)} %bitcast.11, bf16[16,128,128]{2,1,0:T(8,128)(2,1)S(1)} %pad_maximum_fusion.refs_0_, ...), custom_call_target="tpu_custom_call" | custom-call | tf_op jit(solution)/shard_map/pallas_call | solution.py:109
  (10 shorter events, 0.0 us)
Async XLA Ops:
  0.0 29.4 %collective-permute-start.1 = (bf16[2,128,128]{2,1,0:T(8,128)(2,1)}, bf16[2,128,128]{2,1,0:T(8,128)(2,1)S(1)}, u32[]{:S(2)}, u32[]{:S(2)}) collective-permute-start(bf16[2,128,128]{2,1,0:T(8,128)(2,1)} %bitcast.15), channel_id=1, source_target_pairs={{0,512},{256,768},{512,0},{768,256},{1,513},{257,769},{513,1},{769... | collective-permute-start | bytes 196616 | tf_op jit(solution)/shard_map/ppermute | solution.py:18
  15.7 36.3 %collective-permute-start = (bf16[2,128,128]{2,1,0:T(8,128)(2,1)}, bf16[2,128,128]{2,1,0:T(8,128)(2,1)S(1)}, u32[]{:S(2)}, u32[]{:S(2)}) collective-permute-start(bf16[2,128,128]{2,1,0:T(8,128)(2,1)} %bitcast.17), channel_id=1, source_target_pairs={{0,1},{1,0},{2,3},{3,2},{4,5},{5,4},{6,7},{7,6},{8,9},{9,8},{10,11... | collective-permute-start | bytes 196616 | tf_op jit(solution)/shard_map/ppermute | solution.py:18
  30.3 21.7 %copy-start.4 = (bf16[1,2,128,128]{3,2,1,0:T(8,128)(2,1)S(1)}, bf16[1,2,128,128]{3,2,1,0:T(8,128)(2,1)}, u32[]{:S(2)}) copy-start(bf16[1,2,128,128]{3,2,1,0:T(8,128)(2,1)} %param.6) | copy-start | bytes 196612
  30.3 30.6 %collective-permute-start.5 = (bf16[4,128,128]{2,1,0:T(8,128)(2,1)S(1)}, bf16[4,128,128]{2,1,0:T(8,128)(2,1)S(1)}, u32[]{:S(2)}, u32[]{:S(2)}) collective-permute-start(bf16[4,128,128]{2,1,0:T(8,128)(2,1)S(1)} %pair.1), channel_id=1, source_target_pairs={{0,256},{256,0},{512,768},{768,512},{1,257},{257,1},{513,769},{769... | collective-permute-start | bytes 393224 | tf_op jit(solution)/shard_map/ppermute | solution.py:18
  35.7 31.2 %collective-permute-start.4 = (bf16[4,128,128]{2,1,0:T(8,128)(2,1)S(1)}, bf16[4,128,128]{2,1,0:T(8,128)(2,1)S(1)}, u32[]{:S(2)}, u32[]{:S(2)}) collective-permute-start(bf16[4,128,128]{2,1,0:T(8,128)(2,1)S(1)} %pair.1), channel_id=1, source_target_pairs={{0,192},{64,128},{128,64},{192,0},{1,193},{65,129},{129,65},{193,1... | collective-permute-start | bytes 393224 | tf_op jit(solution)/shard_map/ppermute | solution.py:18
  38.7 31.7 %collective-permute-start.3 = (bf16[4,128,128]{2,1,0:T(8,128)(2,1)S(1)}, bf16[4,128,128]{2,1,0:T(8,128)(2,1)S(1)}, u32[]{:S(2)}, u32[]{:S(2)}) collective-permute-start(bf16[4,128,128]{2,1,0:T(8,128)(2,1)S(1)} %pair.1), channel_id=1, source_target_pairs={{0,128},{64,192},{128,0},{192,64},{1,129},{65,193},{129,1},{193,65... | collective-permute-start | bytes 393224 | tf_op jit(solution)/shard_map/ppermute | solution.py:18
  42.9 27.4 %collective-permute-start.2 = (bf16[4,128,128]{2,1,0:T(8,128)(2,1)S(1)}, bf16[4,128,128]{2,1,0:T(8,128)(2,1)S(1)}, u32[]{:S(2)}, u32[]{:S(2)}) collective-permute-start(bf16[4,128,128]{2,1,0:T(8,128)(2,1)S(1)} %pair.1), channel_id=1, source_target_pairs={{0,64},{64,0},{128,192},{192,128},{1,65},{65,1},{129,193},{193,129... | collective-permute-start | bytes 393224 | tf_op jit(solution)/shard_map/ppermute | solution.py:18
  53.9 35.6 %all-to-all-start = ((bf16[16,4,128,128]{3,2,1,0:T(8,128)(2,1)}), bf16[16,4,128,128]{3,2,1,0:T(8,128)(2,1)S(1)}, u32[]{:S(2)}, u32[]{:S(2)}) async-start(bf16[16,4,128,128]{3,2,1,0:T(8,128)(2,1)} %broadcast_in_dim.4), calls=%async_computation | async-start | bytes 4194304 | tf_op jit(solution)/shard_map/all_to_all | solution.py:22
  60.9 28.5 %copy-start = (s32[1,1,64,4]{2,3,1,0:T(4,128)S(1)}, s32[1,1,64,4]{2,3,1,0:T(4,128)}, u32[]{:S(2)}) copy-start(s32[1,1,64,4]{2,3,1,0:T(4,128)} %param.8) | copy-start | bytes 3076
  60.9 28.5 %copy-start.1 = (s32[1,1,64,4]{2,3,1,0:T(4,128)S(1)}, s32[1,1,64,4]{2,3,1,0:T(4,128)}, u32[]{:S(2)}) copy-start(s32[1,1,64,4]{2,3,1,0:T(4,128)} %param.9) | copy-start | bytes 3076
  61.0 28.5 %copy-start.2 = (s32[1,1,64]{2,1,0:T(1,128)S(1)}, s32[1,1,64]{2,1,0:T(1,128)}, u32[]{:S(2)}) copy-start(s32[1,1,64]{2,1,0:T(1,128)} %param.10) | copy-start | bytes 772
  61.0 12.4 %collective-permute-start.8 = (bf16[4,128,128]{2,1,0:T(8,128)(2,1)S(1)}, bf16[4,128,128]{2,1,0:T(8,128)(2,1)S(1)}, u32[]{:S(2)}, u32[]{:S(2)}) collective-permute-start(bf16[4,128,128]{2,1,0:T(8,128)(2,1)S(1)} %rest.1), channel_id=1, source_target_pairs={{0,192},{64,128},{128,64},{192,0},{1,193},{65,129},{129,65},{193,1... | collective-permute-start | bytes 393224 | tf_op jit(solution)/shard_map/ppermute | solution.py:18
  63.0 10.9 %collective-permute-start.7 = (bf16[4,128,128]{2,1,0:T(8,128)(2,1)S(1)}, bf16[4,128,128]{2,1,0:T(8,128)(2,1)S(1)}, u32[]{:S(2)}, u32[]{:S(2)}) collective-permute-start(bf16[4,128,128]{2,1,0:T(8,128)(2,1)S(1)} %rest.1), channel_id=1, source_target_pairs={{0,128},{64,192},{128,0},{192,64},{1,129},{65,193},{129,1},{193,65... | collective-permute-start | bytes 393224 | tf_op jit(solution)/shard_map/ppermute | solution.py:18
  66.9 7.8 %collective-permute-start.6 = (bf16[4,128,128]{2,1,0:T(8,128)(2,1)S(1)}, bf16[4,128,128]{2,1,0:T(8,128)(2,1)S(1)}, u32[]{:S(2)}, u32[]{:S(2)}) collective-permute-start(bf16[4,128,128]{2,1,0:T(8,128)(2,1)S(1)} %rest.1), channel_id=1, source_target_pairs={{0,64},{64,0},{128,192},{192,128},{1,65},{65,1},{129,193},{193,129... | collective-permute-start | bytes 393224 | tf_op jit(solution)/shard_map/ppermute | solution.py:18
  70.4 7.0 %collective-permute-start.9 = (bf16[16,128,128]{2,1,0:T(8,128)(2,1)S(1)}, bf16[16,128,128]{2,1,0:T(8,128)(2,1)S(1)}, u32[]{:S(2)}, u32[]{:S(2)}) collective-permute-start(bf16[16,128,128]{2,1,0:T(8,128)(2,1)S(1)} %pad_maximum_fusion.refs_0_), channel_id=1, source_target_pairs={{0,32},{32,0},{1,33},{33,1},{2,34},{34,2},{3,35},{35,3},{4,36},{36... | collective-permute-start | bytes 1572872 | tf_op jit(solution)/shard_map/ppermute | solution.py:18
  74.8 3.9 %collective-permute-start.10 = (bf16[16,128,128]{2,1,0:T(8,128)(2,1)S(1)}, bf16[16,128,128]{2,1,0:T(8,128)(2,1)}, u32[]{:S(2)}, u32[]{:S(2)}) collective-permute-start(bf16[16,128,128]{2,1,0:T(8,128)(2,1)S(1)} %pad_maximum_fusion.1.refs_1_), channel_id=1, source_target_pairs={{0,32},{32,0},{1,33},{33,1},{2,34},{34,2},{3,35},{35,3},{4,36},{36... | collective-permute-start | bytes 1572872 | tf_op jit(solution)/shard_map/ppermute | solution.py:18
  77.4 0.8 copy-start.3

commit v5 on v4

--- a/solution.py
+++ b/solution.py
@@ -19,7 +19,7 @@
 
 
 def exchange_plane(value):
-    return lax.all_to_all(value, ("y", "x"), split_axis=0, concat_axis=0, tiled=True)
+    return lax.all_to_all(value, ("x", "y"), split_axis=0, concat_axis=0, tiled=True)
 
 
 def hold(value, name, cost=0):
@@ -51,21 +51,11 @@
         right[pl.ds(first, piece.shape[0])] = piece[...]
         first += piece.shape[0]
     out[...] = jnp.zeros_like(out)
-    za, zb, core, half = (lax.axis_index(a) for a in ("za", "zb", "core", "zh"))
     count = counts[0, 0]
 
-    def left_at(slot):
-        return slot ^ (half << 1)
-
-    def right_at(slot):
-        far = (slot >> 4) ^ za
-        near = ((slot >> 2) & 3) ^ zb
-        other = ((slot >> 1) & 1) ^ core
-        return (other << 5) + ((far & 1) << 4) + (near << 2) + (far & 2) + (slot & 1)
-
     def stack_sum(t):
-        lefts = [left[left_at(lefts_at[g, t])] for g in range(4)]
-        rights = [right[right_at(rights_at[g, t])] for g in range(4)]
+        lefts = [left[lefts_at[g, t]] for g in range(4)]
+        rights = [right[rights_at[g, t]] for g in range(4)]
         return jnp.dot(
             jnp.concatenate(lefts, 1),
             jnp.concatenate(rights, 0),
@@ -84,6 +74,16 @@
         return carry
 
     lax.fori_loop(0, lax.div(count + UNROLL - 1, UNROLL), step, 0)
+
+
+def places_of(lefts, rights):
+    za, zb, core, half = (lax.axis_index(a) for a in ("za", "zb", "core", "zh"))
+    left = ((lefts & 12) << 2) + ((lefts >> 4) << 2) + ((lefts & 3) ^ (half << 1))
+    far = (rights >> 4) ^ za
+    near = ((rights >> 2) & 3) ^ zb
+    other = ((rights >> 1) & 1) ^ core
+    right = (other << 5) + ((far & 1) << 4) + (near << 2) + (far & 2) + (rights & 1)
+    return left, right
 
 
 def body(left_values, right_values, stack_left, stack_right, stack_slot, stack_count):
@@ -105,6 +105,8 @@
         pltpu.with_memory_space_constraint(swap(piece, "core", 2, 1), pltpu.HBM)
         for piece in pieces
     ]
+    stack_left, stack_right, late = lax.optimization_barrier((stack_left, stack_right, late))
+    lefts_at, rights_at = places_of(stack_left, stack_right)
     block = own_left.shape[1]
     return pl.pallas_call(
         stacks_kernel,
@@ -119,8 +121,8 @@
         ],
         compiler_params=pltpu.CompilerParams(vmem_limit_bytes=8 << 20),
     )(
-        stack_left[0, 0].T,
-        stack_right[0, 0].T,
+        lefts_at[0, 0].T,
+        rights_at[0, 0].T,
         stack_slot[0, 0],
         stack_count,
         plane.reshape(64, block, block),

time: 94.2 us -> 93.6 us (level)
  no operation moved by 1% of the time
where the time goes in v5:
time: 93.6 us; the launch traced here: 93.1 us
  starting transfers between devices  64.3 us (69%)
  waiting for transfers between devices  20.9 us (22%)
  Pallas kernels  4.1 us (4%)
  local copies, waits for them, and re-layouts  1.88 us (2%)
  other arithmetic  1.02 us (1%)
    ppermute x11, starting transfers between devices, swap(): return lax.ppermute(value, axis, [(i, i ^ bits) for i in range(size)])  57.2 us
    ppermute x11, waiting for transfers between devices, swap(): return lax.ppermute(value, axis, [(i, i ^ bits) for i in range(size)])  10.7 us
    all_to_all x1, waiting for transfers between devices, exchange_plane(): lax.all_to_all(value, ('x', 'y'), split_axis=0, concat_axis=0, tiled=True)  10.2 us
    all_to_all x1, starting transfers between devices, exchange_plane(): lax.all_to_all(value, ('x', 'y'), split_axis=0, concat_axis=0, tiled=True)  7.03 us
    pallas_call x1, Pallas kernels, body(): pl.pallas_call(stacks_kernel, out_shape=jax.ShapeDtypeStruct((CSLOT, bloc...  4.1 us
  transfers between devices with their start and end apart: 12, of which 6 were waited for; matrix products, arithmetic and copies ran while one was open for 3% of the time, Pallas kernels for 0%

profile of v5, /device:TPU:160, one launch (start us, length us, event | category | flops | bytes accessed | tf_op | source)
XLA Modules:
  0.0 93.1 jit_solution(8705272267963849464)
XLA Ops:
  0.0 15.7 %collective-permute-start = (bf16[2,128,128]{2,1,0:T(8,128)(2,1)}, bf16[2,128,128]{2,1,0:T(8,128)(2,1)S(1)}, u32[]{:S(2)}, u32[]{:S(2)}) collective-permute-start(bf16[2,128,128]{2,1,0:T(8,128)(2,1)} %bitcast.15), channel_id=1, source_target_pairs={{0,512},{256,768},{512,0},{768,256},{1,513},{257,769},{513,1},{769... | collective-permute-start | bytes 196616 | tf_op jit(solution)/shard_map/ppermute | solution.py:18
  15.7 13.7 %collective-permute-start.5 = (bf16[2,128,128]{2,1,0:T(8,128)(2,1)}, bf16[2,128,128]{2,1,0:T(8,128)(2,1)S(1)}, u32[]{:S(2)}, u32[]{:S(2)}) collective-permute-start(bf16[2,128,128]{2,1,0:T(8,128)(2,1)} %bitcast.17), channel_id=1, source_target_pairs={{0,1},{1,0},{2,3},{3,2},{4,5},{5,4},{6,7},{7,6},{8,9},{9,8},{10,11... | collective-permute-start | bytes 196616 | tf_op jit(solution)/shard_map/ppermute | solution.py:18
  29.4 0.0 collective-permute-done
  29.4 0.9 pad_maximum_fusion.2.ref
  30.3 0.0 copy-start.1
  30.3 5.5 %collective-permute-start.1 = (bf16[4,128,128]{2,1,0:T(8,128)(2,1)S(1)}, bf16[4,128,128]{2,1,0:T(8,128)(2,1)S(1)}, u32[]{:S(2)}, u32[]{:S(2)}) collective-permute-start(bf16[4,128,128]{2,1,0:T(8,128)(2,1)S(1)} %pair.1), channel_id=1, source_target_pairs={{0,256},{256,0},{512,768},{768,512},{1,257},{257,1},{513,769},{769... | collective-permute-start | bytes 393224 | tf_op jit(solution)/shard_map/ppermute | solution.py:18
  35.7 2.9 %collective-permute-start.8 = (bf16[4,128,128]{2,1,0:T(8,128)(2,1)S(1)}, bf16[4,128,128]{2,1,0:T(8,128)(2,1)S(1)}, u32[]{:S(2)}, u32[]{:S(2)}) collective-permute-start(bf16[4,128,128]{2,1,0:T(8,128)(2,1)S(1)} %pair.1), channel_id=1, source_target_pairs={{0,192},{64,128},{128,64},{192,0},{1,193},{65,129},{129,65},{193,1... | collective-permute-start | bytes 393224 | tf_op jit(solution)/shard_map/ppermute | solution.py:18
  38.7 4.3 %collective-permute-start.7 = (bf16[4,128,128]{2,1,0:T(8,128)(2,1)S(1)}, bf16[4,128,128]{2,1,0:T(8,128)(2,1)S(1)}, u32[]{:S(2)}, u32[]{:S(2)}) collective-permute-start(bf16[4,128,128]{2,1,0:T(8,128)(2,1)S(1)} %pair.1), channel_id=1, source_target_pairs={{0,128},{64,192},{128,0},{192,64},{1,129},{65,193},{129,1},{193,65... | collective-permute-start | bytes 393224 | tf_op jit(solution)/shard_map/ppermute | solution.py:18
  42.9 2.0 %collective-permute-start.6 = (bf16[4,128,128]{2,1,0:T(8,128)(2,1)S(1)}, bf16[4,128,128]{2,1,0:T(8,128)(2,1)S(1)}, u32[]{:S(2)}, u32[]{:S(2)}) collective-permute-start(bf16[4,128,128]{2,1,0:T(8,128)(2,1)S(1)} %pair.1), channel_id=1, source_target_pairs={{0,64},{64,0},{128,192},{192,128},{1,65},{65,1},{129,193},{193,129... | collective-permute-start | bytes 393224 | tf_op jit(solution)/shard_map/ppermute | solution.py:18
  45.0 7.0 %collective-permute-done.5 = bf16[2,128,128]{2,1,0:T(8,128)(2,1)S(1)} collective-permute-done((bf16[2,128,128]{2,1,0:T(8,128)(2,1)}, bf16[2,128,128]{2,1,0:T(8,128)(2,1)S(1)}, u32[]{:S(2)}, u32[]{:S(2)}) %collective-permute-start.5) | collective-permute-done | bytes 65568 | tf_op jit(solution)/shard_map/ppermute | solution.py:18
  52.0 1.9 %broadcast_in_dim.4 = bf16[16,4,128,128]{3,2,1,0:T(8,128)(2,1)} broadcast(bf16[4,128,128]{2,1,0:T(8,128)(2,1)S(1)} %pad_maximum_fusion.3), dimensions={1,2,3} | broadcast | bytes 2228224 | tf_op jit(solution)/shard_map/broadcast_in_dim | solution.py:99
  53.9 7.0 %all-to-all-start = ((bf16[16,4,128,128]{3,2,1,0:T(8,128)(2,1)}), bf16[16,4,128,128]{3,2,1,0:T(8,128)(2,1)S(1)}, u32[]{:S(2)}, u32[]{:S(2)}) async-start(bf16[16,4,128,128]{3,2,1,0:T(8,128)(2,1)} %broadcast_in_dim.4), calls=%async_computation | async-start | bytes 4194304 | tf_op jit(solution)/shard_map/all_to_all | solution.py:22
  60.9 0.0 collective-permute-done.1.ref
  60.9 0.0 copy-start.2
  60.9 0.0 copy-start.3
  61.0 0.0 copy-start
  61.0 2.1 %collective-permute-start.4 = (bf16[4,128,128]{2,1,0:T(8,128)(2,1)S(1)}, bf16[4,128,128]{2,1,0:T(8,128)(2,1)S(1)}, u32[]{:S(2)}, u32[]{:S(2)}) collective-permute-start(bf16[4,128,128]{2,1,0:T(8,128)(2,1)S(1)} %rest.1), channel_id=1, source_target_pairs={{0,192},{64,128},{128,64},{192,0},{1,193},{65,129},{129,65},{193,1... | collective-permute-start | bytes 393224 | tf_op jit(solution)/shard_map/ppermute | solution.py:18
  63.0 3.9 %collective-permute-start.3 = (bf16[4,128,128]{2,1,0:T(8,128)(2,1)S(1)}, bf16[4,128,128]{2,1,0:T(8,128)(2,1)S(1)}, u32[]{:S(2)}, u32[]{:S(2)}) collective-permute-start(bf16[4,128,128]{2,1,0:T(8,128)(2,1)S(1)} %rest.1), channel_id=1, source_target_pairs={{0,128},{64,192},{128,0},{192,64},{1,129},{65,193},{129,1},{193,65... | collective-permute-start | bytes 393224 | tf_op jit(solution)/shard_map/ppermute | solution.py:18
  66.9 0.0 collective-permute-done.8
  66.9 3.4 %collective-permute-start.2 = (bf16[4,128,128]{2,1,0:T(8,128)(2,1)S(1)}, bf16[4,128,128]{2,1,0:T(8,128)(2,1)S(1)}, u32[]{:S(2)}, u32[]{:S(2)}) collective-permute-start(bf16[4,128,128]{2,1,0:T(8,128)(2,1)S(1)} %rest.1), channel_id=1, source_target_pairs={{0,64},{64,0},{128,192},{192,128},{1,65},{65,1},{129,193},{193,129... | collective-permute-start | bytes 393224 | tf_op jit(solution)/shard_map/ppermute | solution.py:18
  70.3 0.0 collective-permute-done.7
  70.4 0.0 collective-permute-done.6
  70.4 0.1 pad_maximum_fusion.1.refs_0_
  70.4 1.9 %collective-permute-start.9 = (bf16[16,128,128]{2,1,0:T(8,128)(2,1)S(1)}, bf16[16,128,128]{2,1,0:T(8,128)(2,1)}, u32[]{:S(2)}, u32[]{:S(2)}) collective-permute-start(bf16[16,128,128]{2,1,0:T(8,128)(2,1)S(1)} %pad_maximum_fusion.1.refs_0_), channel_id=1, source_target_pairs={{0,32},{32,0},{1,33},{33,1},{2,34},{34,2},{3,35},{35,3},{4,36},{36... | collective-permute-start | bytes 1572872 | tf_op jit(solution)/shard_map/ppermute | solution.py:18
  72.4 1.0 %collective-permute-done.4 = bf16[4,128,128]{2,1,0:T(8,128)(2,1)S(1)} collective-permute-done((bf16[4,128,128]{2,1,0:T(8,128)(2,1)S(1)}, bf16[4,128,128]{2,1,0:T(8,128)(2,1)S(1)}, u32[]{:S(2)}, u32[]{:S(2)}) %collective-permute-start.4) | collective-permute-done | bytes 131104 | tf_op jit(solution)/shard_map/ppermute | solution.py:18
  73.4 0.5 collective-permute-done.3
  73.9 0.8 collective-permute-done.2
  74.8 0.1 pad_maximum_fusion.refs_1_
  74.8 1.9 %collective-permute-start.10 = (bf16[16,128,128]{2,1,0:T(8,128)(2,1)S(1)}, bf16[16,128,128]{2,1,0:T(8,128)(2,1)}, u32[]{:S(2)}, u32[]{:S(2)}) collective-permute-start(bf16[16,128,128]{2,1,0:T(8,128)(2,1)S(1)} %pad_maximum_fusion.refs_1_), channel_id=1, source_target_pairs={{0,32},{32,0},{1,33},{33,1},{2,34},{34,2},{3,35},{35,3},{4,36},{36... | collective-permute-start | bytes 1572872 | tf_op jit(solution)/shard_map/ppermute | solution.py:18
  77.5 1.3 %collective-permute-done.10.refs_3_ = bf16[16,128,128]{2,1,0:T(8,128)(2,1)} collective-permute-done((bf16[16,128,128]{2,1,0:T(8,128)(2,1)S(1)}, bf16[16,128,128]{2,1,0:T(8,128)(2,1)}, u32[]{:S(2)}, u32[]{:S(2)}) %collective-permute-start.10) | collective-permute-done | bytes 524320 | tf_op jit(solution)/shard_map/ppermute | solution.py:18
  78.8 10.2 %all-to-all-done = bf16[16,4,128,128]{3,2,1,0:T(8,128)(2,1)S(1)} async-done(((bf16[16,4,128,128]{3,2,1,0:T(8,128)(2,1)}), bf16[16,4,128,128]{3,2,1,0:T(8,128)(2,1)S(1)}, u32[]{:S(2)}, u32[]{:S(2)}) %all-to-all-start) | async-done | bytes 2097184 | tf_op jit(solution)/shard_map/all_to_all | solution.py:22
  89.0 4.1 %shard_map.64 = f32[8,128,128]{2,1,0:T(8,128)} custom-call(s32[4,64]{1,0:T(4,128)S(1)} %get-tuple-element.10.lefts_at, s32[4,64]{1,0:T(4,128)S(1)} %get-tuple-element.9.rights_at, s32[64]{0:T(128)S(1)} %bitcast.14, s32[1,1]{1,0:T(1,128)S(6)} %copy.11.counts, bf16[64,128,128]{2,1,0:T(8,128)(2,1)S(1)} %bitcast.13, ...), custom_call_target="tpu_custom_call" | custom-call | tf_op jit(solution)/shard_map/pallas_call | solution.py:111
  (9 shorter events, 0.0 us)
Async XLA Ops:
  0.0 29.4 %collective-permute-start = (bf16[2,128,128]{2,1,0:T(8,128)(2,1)}, bf16[2,128,128]{2,1,0:T(8,128)(2,1)S(1)}, u32[]{:S(2)}, u32[]{:S(2)}) collective-permute-start(bf16[2,128,128]{2,1,0:T(8,128)(2,1)} %bitcast.15), channel_id=1, source_target_pairs={{0,512},{256,768},{512,0},{768,256},{1,513},{257,769},{513,1},{769... | collective-permute-start | bytes 196616 | tf_op jit(solution)/shard_map/ppermute | solution.py:18
  15.7 36.3 %collective-permute-start.5 = (bf16[2,128,128]{2,1,0:T(8,128)(2,1)}, bf16[2,128,128]{2,1,0:T(8,128)(2,1)S(1)}, u32[]{:S(2)}, u32[]{:S(2)}) collective-permute-start(bf16[2,128,128]{2,1,0:T(8,128)(2,1)} %bitcast.17), channel_id=1, source_target_pairs={{0,1},{1,0},{2,3},{3,2},{4,5},{5,4},{6,7},{7,6},{8,9},{9,8},{10,11... | collective-permute-start | bytes 196616 | tf_op jit(solution)/shard_map/ppermute | solution.py:18
  30.3 21.7 %copy-start.1 = (bf16[1,2,128,128]{3,2,1,0:T(8,128)(2,1)S(1)}, bf16[1,2,128,128]{3,2,1,0:T(8,128)(2,1)}, u32[]{:S(2)}) copy-start(bf16[1,2,128,128]{3,2,1,0:T(8,128)(2,1)} %param.6) | copy-start | bytes 196612
  30.3 30.6 %collective-permute-start.1 = (bf16[4,128,128]{2,1,0:T(8,128)(2,1)S(1)}, bf16[4,128,128]{2,1,0:T(8,128)(2,1)S(1)}, u32[]{:S(2)}, u32[]{:S(2)}) collective-permute-start(bf16[4,128,128]{2,1,0:T(8,128)(2,1)S(1)} %pair.1), channel_id=1, source_target_pairs={{0,256},{256,0},{512,768},{768,512},{1,257},{257,1},{513,769},{769... | collective-permute-start | bytes 393224 | tf_op jit(solution)/shard_map/ppermute | solution.py:18
  35.7 31.2 %collective-permute-start.8 = (bf16[4,128,128]{2,1,0:T(8,128)(2,1)S(1)}, bf16[4,128,128]{2,1,0:T(8,128)(2,1)S(1)}, u32[]{:S(2)}, u32[]{:S(2)}) collective-permute-start(bf16[4,128,128]{2,1,0:T(8,128)(2,1)S(1)} %pair.1), channel_id=1, source_target_pairs={{0,192},{64,128},{128,64},{192,0},{1,193},{65,129},{129,65},{193,1... | collective-permute-start | bytes 393224 | tf_op jit(solution)/shard_map/ppermute | solution.py:18
  38.7 31.7 %collective-permute-start.7 = (bf16[4,128,128]{2,1,0:T(8,128)(2,1)S(1)}, bf16[4,128,128]{2,1,0:T(8,128)(2,1)S(1)}, u32[]{:S(2)}, u32[]{:S(2)}) collective-permute-start(bf16[4,128,128]{2,1,0:T(8,128)(2,1)S(1)} %pair.1), channel_id=1, source_target_pairs={{0,128},{64,192},{128,0},{192,64},{1,129},{65,193},{129,1},{193,65... | collective-permute-start | bytes 393224 | tf_op jit(solution)/shard_map/ppermute | solution.py:18
  42.9 27.4 %collective-permute-start.6 = (bf16[4,128,128]{2,1,0:T(8,128)(2,1)S(1)}, bf16[4,128,128]{2,1,0:T(8,128)(2,1)S(1)}, u32[]{:S(2)}, u32[]{:S(2)}) collective-permute-start(bf16[4,128,128]{2,1,0:T(8,128)(2,1)S(1)} %pair.1), channel_id=1, source_target_pairs={{0,64},{64,0},{128,192},{192,128},{1,65},{65,1},{129,193},{193,129... | collective-permute-start | bytes 393224 | tf_op jit(solution)/shard_map/ppermute | solution.py:18
  53.9 35.1 %all-to-all-start = ((bf16[16,4,128,128]{3,2,1,0:T(8,128)(2,1)}), bf16[16,4,128,128]{3,2,1,0:T(8,128)(2,1)S(1)}, u32[]{:S(2)}, u32[]{:S(2)}) async-start(bf16[16,4,128,128]{3,2,1,0:T(8,128)(2,1)} %broadcast_in_dim.4), calls=%async_computation | async-start | bytes 4194304 | tf_op jit(solution)/shard_map/all_to_all | solution.py:22
  60.9 16.5 %copy-start.2 = (s32[1,1,64,4]{2,3,1,0:T(4,128)S(1)}, s32[1,1,64,4]{2,3,1,0:T(4,128)}, u32[]{:S(2)}) copy-start(s32[1,1,64,4]{2,3,1,0:T(4,128)} %param.9) | copy-start | bytes 3076
  60.9 16.5 %copy-start.3 = (s32[1,1,64,4]{2,3,1,0:T(4,128)S(1)}, s32[1,1,64,4]{2,3,1,0:T(4,128)}, u32[]{:S(2)}) copy-start(s32[1,1,64,4]{2,3,1,0:T(4,128)} %param.8) | copy-start | bytes 3076
  61.0 28.0 %copy-start = (s32[1,1,64]{2,1,0:T(1,128)S(1)}, s32[1,1,64]{2,1,0:T(1,128)}, u32[]{:S(2)}) copy-start(s32[1,1,64]{2,1,0:T(1,128)} %param.10) | copy-start | bytes 772
  61.0 12.4 %collective-permute-start.4 = (bf16[4,128,128]{2,1,0:T(8,128)(2,1)S(1)}, bf16[4,128,128]{2,1,0:T(8,128)(2,1)S(1)}, u32[]{:S(2)}, u32[]{:S(2)}) collective-permute-start(bf16[4,128,128]{2,1,0:T(8,128)(2,1)S(1)} %rest.1), channel_id=1, source_target_pairs={{0,192},{64,128},{128,64},{192,0},{1,193},{65,129},{129,65},{193,1... | collective-permute-start | bytes 393224 | tf_op jit(solution)/shard_map/ppermute | solution.py:18
  63.0 10.9 %collective-permute-start.3 = (bf16[4,128,128]{2,1,0:T(8,128)(2,1)S(1)}, bf16[4,128,128]{2,1,0:T(8,128)(2,1)S(1)}, u32[]{:S(2)}, u32[]{:S(2)}) collective-permute-start(bf16[4,128,128]{2,1,0:T(8,128)(2,1)S(1)} %rest.1), channel_id=1, source_target_pairs={{0,128},{64,192},{128,0},{192,64},{1,129},{65,193},{129,1},{193,65... | collective-permute-start | bytes 393224 | tf_op jit(solution)/shard_map/ppermute | solution.py:18
  66.9 7.8 %collective-permute-start.2 = (bf16[4,128,128]{2,1,0:T(8,128)(2,1)S(1)}, bf16[4,128,128]{2,1,0:T(8,128)(2,1)S(1)}, u32[]{:S(2)}, u32[]{:S(2)}) collective-permute-start(bf16[4,128,128]{2,1,0:T(8,128)(2,1)S(1)} %rest.1), channel_id=1, source_target_pairs={{0,64},{64,0},{128,192},{192,128},{1,65},{65,1},{129,193},{193,129... | collective-permute-start | bytes 393224 | tf_op jit(solution)/shard_map/ppermute | solution.py:18
  70.4 7.0 %collective-permute-start.9 = (bf16[16,128,128]{2,1,0:T(8,128)(2,1)S(1)}, bf16[16,128,128]{2,1,0:T(8,128)(2,1)}, u32[]{:S(2)}, u32[]{:S(2)}) collective-permute-start(bf16[16,128,128]{2,1,0:T(8,128)(2,1)S(1)} %pad_maximum_fusion.1.refs_0_), channel_id=1, source_target_pairs={{0,32},{32,0},{1,33},{33,1},{2,34},{34,2},{3,35},{35,3},{4,36},{36... | collective-permute-start | bytes 1572872 | tf_op jit(solution)/shard_map/ppermute | solution.py:18
  74.8 3.9 %collective-permute-start.10 = (bf16[16,128,128]{2,1,0:T(8,128)(2,1)S(1)}, bf16[16,128,128]{2,1,0:T(8,128)(2,1)}, u32[]{:S(2)}, u32[]{:S(2)}) collective-permute-start(bf16[16,128,128]{2,1,0:T(8,128)(2,1)S(1)} %pad_maximum_fusion.refs_1_), channel_id=1, source_target_pairs={{0,32},{32,0},{1,33},{33,1},{2,34},{34,2},{3,35},{35,3},{4,36},{36... | collective-permute-start | bytes 1572872 | tf_op jit(solution)/shard_map/ppermute | solution.py:18

commit v6 on v5

--- a/solution.py
+++ b/solution.py
@@ -7,7 +7,7 @@
 from jax.sharding import PartitionSpec as P
 
 CSLOT = 8
-UNROLL = 16
+UNROLL = 32
 Z_HI, Z_LO = 4, 4
 AXES = ("za", "zb", "core", "y", "x", "zh")
 SIZES = (Z_HI, Z_LO, 2, 4, 4, 2)

time: 93.6 us -> 93.5 us (level)
  no operation moved by 1% of the time
where the time goes in v6:
time: 93.5 us; the launch traced here: 92.9 us
  starting transfers between devices  64.3 us (69%)
  waiting for transfers between devices  20.9 us (22%)
  Pallas kernels  3.95 us (4%)
  local copies, waits for them, and re-layouts  1.88 us (2%)
  other arithmetic  1.02 us (1%)
    ppermute x11, starting transfers between devices, swap(): return lax.ppermute(value, axis, [(i, i ^ bits) for i in range(size)])  57.2 us
    ppermute x11, waiting for transfers between devices, swap(): return lax.ppermute(value, axis, [(i, i ^ bits) for i in range(size)])  10.7 us
    all_to_all x1, waiting for transfers between devices, exchange_plane(): lax.all_to_all(value, ('x', 'y'), split_axis=0, concat_axis=0, tiled=True)  10.2 us
    all_to_all x1, starting transfers between devices, exchange_plane(): lax.all_to_all(value, ('x', 'y'), split_axis=0, concat_axis=0, tiled=True)  7.03 us
    pallas_call x1, Pallas kernels, body(): pl.pallas_call(stacks_kernel, out_shape=jax.ShapeDtypeStruct((CSLOT, bloc...  3.95 us
  transfers between devices with their start and end apart: 12, of which 6 were waited for; matrix products, arithmetic and copies ran while one was open for 3% of the time, Pallas kernels for 0%

profile of v6, /device:TPU:160, one launch (start us, length us, event | category | flops | bytes accessed | tf_op | source)
XLA Modules:
  0.0 92.9 jit_solution(9753127320110498801)
XLA Ops:
  0.0 15.7 %collective-permute-start = (bf16[2,128,128]{2,1,0:T(8,128)(2,1)}, bf16[2,128,128]{2,1,0:T(8,128)(2,1)S(1)}, u32[]{:S(2)}, u32[]{:S(2)}) collective-permute-start(bf16[2,128,128]{2,1,0:T(8,128)(2,1)} %bitcast.15), channel_id=1, source_target_pairs={{0,512},{256,768},{512,0},{768,256},{1,513},{257,769},{513,1},{769... | collective-permute-start | bytes 196616 | tf_op jit(solution)/shard_map/ppermute | solution.py:18
  15.7 13.7 %collective-permute-start.5 = (bf16[2,128,128]{2,1,0:T(8,128)(2,1)}, bf16[2,128,128]{2,1,0:T(8,128)(2,1)S(1)}, u32[]{:S(2)}, u32[]{:S(2)}) collective-permute-start(bf16[2,128,128]{2,1,0:T(8,128)(2,1)} %bitcast.17), channel_id=1, source_target_pairs={{0,1},{1,0},{2,3},{3,2},{4,5},{5,4},{6,7},{7,6},{8,9},{9,8},{10,11... | collective-permute-start | bytes 196616 | tf_op jit(solution)/shard_map/ppermute | solution.py:18
  29.4 0.0 collective-permute-done
  29.4 0.9 pad_maximum_fusion.2.ref
  30.3 0.0 copy-start.1
  30.3 5.5 %collective-permute-start.1 = (bf16[4,128,128]{2,1,0:T(8,128)(2,1)S(1)}, bf16[4,128,128]{2,1,0:T(8,128)(2,1)S(1)}, u32[]{:S(2)}, u32[]{:S(2)}) collective-permute-start(bf16[4,128,128]{2,1,0:T(8,128)(2,1)S(1)} %pair.1), channel_id=1, source_target_pairs={{0,256},{256,0},{512,768},{768,512},{1,257},{257,1},{513,769},{769... | collective-permute-start | bytes 393224 | tf_op jit(solution)/shard_map/ppermute | solution.py:18
  35.7 2.9 %collective-permute-start.8 = (bf16[4,128,128]{2,1,0:T(8,128)(2,1)S(1)}, bf16[4,128,128]{2,1,0:T(8,128)(2,1)S(1)}, u32[]{:S(2)}, u32[]{:S(2)}) collective-permute-start(bf16[4,128,128]{2,1,0:T(8,128)(2,1)S(1)} %pair.1), channel_id=1, source_target_pairs={{0,192},{64,128},{128,64},{192,0},{1,193},{65,129},{129,65},{193,1... | collective-permute-start | bytes 393224 | tf_op jit(solution)/shard_map/ppermute | solution.py:18
  38.7 4.3 %collective-permute-start.7 = (bf16[4,128,128]{2,1,0:T(8,128)(2,1)S(1)}, bf16[4,128,128]{2,1,0:T(8,128)(2,1)S(1)}, u32[]{:S(2)}, u32[]{:S(2)}) collective-permute-start(bf16[4,128,128]{2,1,0:T(8,128)(2,1)S(1)} %pair.1), channel_id=1, source_target_pairs={{0,128},{64,192},{128,0},{192,64},{1,129},{65,193},{129,1},{193,65... | collective-permute-start | bytes 393224 | tf_op jit(solution)/shard_map/ppermute | solution.py:18
  42.9 2.0 %collective-permute-start.6 = (bf16[4,128,128]{2,1,0:T(8,128)(2,1)S(1)}, bf16[4,128,128]{2,1,0:T(8,128)(2,1)S(1)}, u32[]{:S(2)}, u32[]{:S(2)}) collective-permute-start(bf16[4,128,128]{2,1,0:T(8,128)(2,1)S(1)} %pair.1), channel_id=1, source_target_pairs={{0,64},{64,0},{128,192},{192,128},{1,65},{65,1},{129,193},{193,129... | collective-permute-start | bytes 393224 | tf_op jit(solution)/shard_map/ppermute | solution.py:18
  45.0 7.0 %collective-permute-done.5 = bf16[2,128,128]{2,1,0:T(8,128)(2,1)S(1)} collective-permute-done((bf16[2,128,128]{2,1,0:T(8,128)(2,1)}, bf16[2,128,128]{2,1,0:T(8,128)(2,1)S(1)}, u32[]{:S(2)}, u32[]{:S(2)}) %collective-permute-start.5) | collective-permute-done | bytes 65568 | tf_op jit(solution)/shard_map/ppermute | solution.py:18
  52.0 1.9 %broadcast_in_dim.4 = bf16[16,4,128,128]{3,2,1,0:T(8,128)(2,1)} broadcast(bf16[4,128,128]{2,1,0:T(8,128)(2,1)S(1)} %pad_maximum_fusion.3), dimensions={1,2,3} | broadcast | bytes 2228224 | tf_op jit(solution)/shard_map/broadcast_in_dim | solution.py:99
  53.9 7.0 %all-to-all-start = ((bf16[16,4,128,128]{3,2,1,0:T(8,128)(2,1)}), bf16[16,4,128,128]{3,2,1,0:T(8,128)(2,1)S(1)}, u32[]{:S(2)}, u32[]{:S(2)}) async-start(bf16[16,4,128,128]{3,2,1,0:T(8,128)(2,1)} %broadcast_in_dim.4), calls=%async_computation | async-start | bytes 4194304 | tf_op jit(solution)/shard_map/all_to_all | solution.py:22
  60.9 0.0 collective-permute-done.1.ref
  60.9 0.0 copy-start.2
  60.9 0.0 copy-start.3
  61.0 0.0 copy-start
  61.0 2.1 %collective-permute-start.4 = (bf16[4,128,128]{2,1,0:T(8,128)(2,1)S(1)}, bf16[4,128,128]{2,1,0:T(8,128)(2,1)S(1)}, u32[]{:S(2)}, u32[]{:S(2)}) collective-permute-start(bf16[4,128,128]{2,1,0:T(8,128)(2,1)S(1)} %rest.1), channel_id=1, source_target_pairs={{0,192},{64,128},{128,64},{192,0},{1,193},{65,129},{129,65},{193,1... | collective-permute-start | bytes 393224 | tf_op jit(solution)/shard_map/ppermute | solution.py:18
  63.0 3.9 %collective-permute-start.3 = (bf16[4,128,128]{2,1,0:T(8,128)(2,1)S(1)}, bf16[4,128,128]{2,1,0:T(8,128)(2,1)S(1)}, u32[]{:S(2)}, u32[]{:S(2)}) collective-permute-start(bf16[4,128,128]{2,1,0:T(8,128)(2,1)S(1)} %rest.1), channel_id=1, source_target_pairs={{0,128},{64,192},{128,0},{192,64},{1,129},{65,193},{129,1},{193,65... | collective-permute-start | bytes 393224 | tf_op jit(solution)/shard_map/ppermute | solution.py:18
  66.9 0.0 collective-permute-done.8
  66.9 3.4 %collective-permute-start.2 = (bf16[4,128,128]{2,1,0:T(8,128)(2,1)S(1)}, bf16[4,128,128]{2,1,0:T(8,128)(2,1)S(1)}, u32[]{:S(2)}, u32[]{:S(2)}) collective-permute-start(bf16[4,128,128]{2,1,0:T(8,128)(2,1)S(1)} %rest.1), channel_id=1, source_target_pairs={{0,64},{64,0},{128,192},{192,128},{1,65},{65,1},{129,193},{193,129... | collective-permute-start | bytes 393224 | tf_op jit(solution)/shard_map/ppermute | solution.py:18
  70.3 0.0 collective-permute-done.7
  70.4 0.0 collective-permute-done.6
  70.4 0.1 pad_maximum_fusion.1.refs_0_
  70.4 1.9 %collective-permute-start.9 = (bf16[16,128,128]{2,1,0:T(8,128)(2,1)S(1)}, bf16[16,128,128]{2,1,0:T(8,128)(2,1)}, u32[]{:S(2)}, u32[]{:S(2)}) collective-permute-start(bf16[16,128,128]{2,1,0:T(8,128)(2,1)S(1)} %pad_maximum_fusion.1.refs_0_), channel_id=1, source_target_pairs={{0,32},{32,0},{1,33},{33,1},{2,34},{34,2},{3,35},{35,3},{4,36},{36... | collective-permute-start | bytes 1572872 | tf_op jit(solution)/shard_map/ppermute | solution.py:18
  72.4 1.0 %collective-permute-done.4 = bf16[4,128,128]{2,1,0:T(8,128)(2,1)S(1)} collective-permute-done((bf16[4,128,128]{2,1,0:T(8,128)(2,1)S(1)}, bf16[4,128,128]{2,1,0:T(8,128)(2,1)S(1)}, u32[]{:S(2)}, u32[]{:S(2)}) %collective-permute-start.4) | collective-permute-done | bytes 131104 | tf_op jit(solution)/shard_map/ppermute | solution.py:18
  73.4 0.5 collective-permute-done.3
  73.9 0.8 collective-permute-done.2
  74.8 0.1 pad_maximum_fusion.refs_1_
  74.8 1.9 %collective-permute-start.10 = (bf16[16,128,128]{2,1,0:T(8,128)(2,1)S(1)}, bf16[16,128,128]{2,1,0:T(8,128)(2,1)}, u32[]{:S(2)}, u32[]{:S(2)}) collective-permute-start(bf16[16,128,128]{2,1,0:T(8,128)(2,1)S(1)} %pad_maximum_fusion.refs_1_), channel_id=1, source_target_pairs={{0,32},{32,0},{1,33},{33,1},{2,34},{34,2},{3,35},{35,3},{4,36},{36... | collective-permute-start | bytes 1572872 | tf_op jit(solution)/shard_map/ppermute | solution.py:18
  77.5 1.3 %collective-permute-done.10.refs_3_ = bf16[16,128,128]{2,1,0:T(8,128)(2,1)} collective-permute-done((bf16[16,128,128]{2,1,0:T(8,128)(2,1)S(1)}, bf16[16,128,128]{2,1,0:T(8,128)(2,1)}, u32[]{:S(2)}, u32[]{:S(2)}) %collective-permute-start.10) | collective-permute-done | bytes 524320 | tf_op jit(solution)/shard_map/ppermute | solution.py:18
  78.8 10.2 %all-to-all-done = bf16[16,4,128,128]{3,2,1,0:T(8,128)(2,1)S(1)} async-done(((bf16[16,4,128,128]{3,2,1,0:T(8,128)(2,1)}), bf16[16,4,128,128]{3,2,1,0:T(8,128)(2,1)S(1)}, u32[]{:S(2)}, u32[]{:S(2)}) %all-to-all-start) | async-done | bytes 2097184 | tf_op jit(solution)/shard_map/all_to_all | solution.py:22
  89.0 3.9 %shard_map.64 = f32[8,128,128]{2,1,0:T(8,128)} custom-call(s32[4,64]{1,0:T(4,128)S(1)} %get-tuple-element.10.lefts_at, s32[4,64]{1,0:T(4,128)S(1)} %get-tuple-element.9.rights_at, s32[64]{0:T(128)S(1)} %bitcast.14, s32[1,1]{1,0:T(1,128)S(6)} %copy.11.counts, bf16[64,128,128]{2,1,0:T(8,128)(2,1)S(1)} %bitcast.13, ...), custom_call_target="tpu_custom_call" | custom-call | tf_op jit(solution)/shard_map/pallas_call | solution.py:111
  (9 shorter events, 0.0 us)
Async XLA Ops:
  0.0 29.4 %collective-permute-start = (bf16[2,128,128]{2,1,0:T(8,128)(2,1)}, bf16[2,128,128]{2,1,0:T(8,128)(2,1)S(1)}, u32[]{:S(2)}, u32[]{:S(2)}) collective-permute-start(bf16[2,128,128]{2,1,0:T(8,128)(2,1)} %bitcast.15), channel_id=1, source_target_pairs={{0,512},{256,768},{512,0},{768,256},{1,513},{257,769},{513,1},{769... | collective-permute-start | bytes 196616 | tf_op jit(solution)/shard_map/ppermute | solution.py:18
  15.7 36.3 %collective-permute-start.5 = (bf16[2,128,128]{2,1,0:T(8,128)(2,1)}, bf16[2,128,128]{2,1,0:T(8,128)(2,1)S(1)}, u32[]{:S(2)}, u32[]{:S(2)}) collective-permute-start(bf16[2,128,128]{2,1,0:T(8,128)(2,1)} %bitcast.17), channel_id=1, source_target_pairs={{0,1},{1,0},{2,3},{3,2},{4,5},{5,4},{6,7},{7,6},{8,9},{9,8},{10,11... | collective-permute-start | bytes 196616 | tf_op jit(solution)/shard_map/ppermute | solution.py:18
  30.3 21.7 %copy-start.1 = (bf16[1,2,128,128]{3,2,1,0:T(8,128)(2,1)S(1)}, bf16[1,2,128,128]{3,2,1,0:T(8,128)(2,1)}, u32[]{:S(2)}) copy-start(bf16[1,2,128,128]{3,2,1,0:T(8,128)(2,1)} %param.6) | copy-start | bytes 196612
  30.3 30.6 %collective-permute-start.1 = (bf16[4,128,128]{2,1,0:T(8,128)(2,1)S(1)}, bf16[4,128,128]{2,1,0:T(8,128)(2,1)S(1)}, u32[]{:S(2)}, u32[]{:S(2)}) collective-permute-start(bf16[4,128,128]{2,1,0:T(8,128)(2,1)S(1)} %pair.1), channel_id=1, source_target_pairs={{0,256},{256,0},{512,768},{768,512},{1,257},{257,1},{513,769},{769... | collective-permute-start | bytes 393224 | tf_op jit(solution)/shard_map/ppermute | solution.py:18
  35.7 31.2 %collective-permute-start.8 = (bf16[4,128,128]{2,1,0:T(8,128)(2,1)S(1)}, bf16[4,128,128]{2,1,0:T(8,128)(2,1)S(1)}, u32[]{:S(2)}, u32[]{:S(2)}) collective-permute-start(bf16[4,128,128]{2,1,0:T(8,128)(2,1)S(1)} %pair.1), channel_id=1, source_target_pairs={{0,192},{64,128},{128,64},{192,0},{1,193},{65,129},{129,65},{193,1... | collective-permute-start | bytes 393224 | tf_op jit(solution)/shard_map/ppermute | solution.py:18
  38.7 31.7 %collective-permute-start.7 = (bf16[4,128,128]{2,1,0:T(8,128)(2,1)S(1)}, bf16[4,128,128]{2,1,0:T(8,128)(2,1)S(1)}, u32[]{:S(2)}, u32[]{:S(2)}) collective-permute-start(bf16[4,128,128]{2,1,0:T(8,128)(2,1)S(1)} %pair.1), channel_id=1, source_target_pairs={{0,128},{64,192},{128,0},{192,64},{1,129},{65,193},{129,1},{193,65... | collective-permute-start | bytes 393224 | tf_op jit(solution)/shard_map/ppermute | solution.py:18
  42.9 27.4 %collective-permute-start.6 = (bf16[4,128,128]{2,1,0:T(8,128)(2,1)S(1)}, bf16[4,128,128]{2,1,0:T(8,128)(2,1)S(1)}, u32[]{:S(2)}, u32[]{:S(2)}) collective-permute-start(bf16[4,128,128]{2,1,0:T(8,128)(2,1)S(1)} %pair.1), channel_id=1, source_target_pairs={{0,64},{64,0},{128,192},{192,128},{1,65},{65,1},{129,193},{193,129... | collective-permute-start | bytes 393224 | tf_op jit(solution)/shard_map/ppermute | solution.py:18
  53.9 35.1 %all-to-all-start = ((bf16[16,4,128,128]{3,2,1,0:T(8,128)(2,1)}), bf16[16,4,128,128]{3,2,1,0:T(8,128)(2,1)S(1)}, u32[]{:S(2)}, u32[]{:S(2)}) async-start(bf16[16,4,128,128]{3,2,1,0:T(8,128)(2,1)} %broadcast_in_dim.4), calls=%async_computation | async-start | bytes 4194304 | tf_op jit(solution)/shard_map/all_to_all | solution.py:22
  60.9 16.5 %copy-start.2 = (s32[1,1,64,4]{2,3,1,0:T(4,128)S(1)}, s32[1,1,64,4]{2,3,1,0:T(4,128)}, u32[]{:S(2)}) copy-start(s32[1,1,64,4]{2,3,1,0:T(4,128)} %param.9) | copy-start | bytes 3076
  60.9 16.5 %copy-start.3 = (s32[1,1,64,4]{2,3,1,0:T(4,128)S(1)}, s32[1,1,64,4]{2,3,1,0:T(4,128)}, u32[]{:S(2)}) copy-start(s32[1,1,64,4]{2,3,1,0:T(4,128)} %param.8) | copy-start | bytes 3076
  61.0 28.0 %copy-start = (s32[1,1,64]{2,1,0:T(1,128)S(1)}, s32[1,1,64]{2,1,0:T(1,128)}, u32[]{:S(2)}) copy-start(s32[1,1,64]{2,1,0:T(1,128)} %param.10) | copy-start | bytes 772
  61.0 12.4 %collective-permute-start.4 = (bf16[4,128,128]{2,1,0:T(8,128)(2,1)S(1)}, bf16[4,128,128]{2,1,0:T(8,128)(2,1)S(1)}, u32[]{:S(2)}, u32[]{:S(2)}) collective-permute-start(bf16[4,128,128]{2,1,0:T(8,128)(2,1)S(1)} %rest.1), channel_id=1, source_target_pairs={{0,192},{64,128},{128,64},{192,0},{1,193},{65,129},{129,65},{193,1... | collective-permute-start | bytes 393224 | tf_op jit(solution)/shard_map/ppermute | solution.py:18
  63.0 10.9 %collective-permute-start.3 = (bf16[4,128,128]{2,1,0:T(8,128)(2,1)S(1)}, bf16[4,128,128]{2,1,0:T(8,128)(2,1)S(1)}, u32[]{:S(2)}, u32[]{:S(2)}) collective-permute-start(bf16[4,128,128]{2,1,0:T(8,128)(2,1)S(1)} %rest.1), channel_id=1, source_target_pairs={{0,128},{64,192},{128,0},{192,64},{1,129},{65,193},{129,1},{193,65... | collective-permute-start | bytes 393224 | tf_op jit(solution)/shard_map/ppermute | solution.py:18
  66.9 7.8 %collective-permute-start.2 = (bf16[4,128,128]{2,1,0:T(8,128)(2,1)S(1)}, bf16[4,128,128]{2,1,0:T(8,128)(2,1)S(1)}, u32[]{:S(2)}, u32[]{:S(2)}) collective-permute-start(bf16[4,128,128]{2,1,0:T(8,128)(2,1)S(1)} %rest.1), channel_id=1, source_target_pairs={{0,64},{64,0},{128,192},{192,128},{1,65},{65,1},{129,193},{193,129... | collective-permute-start | bytes 393224 | tf_op jit(solution)/shard_map/ppermute | solution.py:18
  70.4 7.0 %collective-permute-start.9 = (bf16[16,128,128]{2,1,0:T(8,128)(2,1)S(1)}, bf16[16,128,128]{2,1,0:T(8,128)(2,1)}, u32[]{:S(2)}, u32[]{:S(2)}) collective-permute-start(bf16[16,128,128]{2,1,0:T(8,128)(2,1)S(1)} %pad_maximum_fusion.1.refs_0_), channel_id=1, source_target_pairs={{0,32},{32,0},{1,33},{33,1},{2,34},{34,2},{3,35},{35,3},{4,36},{36... | collective-permute-start | bytes 1572872 | tf_op jit(solution)/shard_map/ppermute | solution.py:18
  74.8 3.9 %collective-permute-start.10 = (bf16[16,128,128]{2,1,0:T(8,128)(2,1)S(1)}, bf16[16,128,128]{2,1,0:T(8,128)(2,1)}, u32[]{:S(2)}, u32[]{:S(2)}) collective-permute-start(bf16[16,128,128]{2,1,0:T(8,128)(2,1)S(1)} %pad_maximum_fusion.refs_1_), channel_id=1, source_target_pairs={{0,32},{32,0},{1,33},{33,1},{2,34},{34,2},{3,35},{35,3},{4,36},{36... | collective-permute-start | bytes 1572872 | tf_op jit(solution)/shard_map/ppermute | solution.py:18
